TPU v7x, 32 devices: a whole 2x2x4 slice. The times are simulated.
32 devices in a mesh: dp: 8 (over z, x), tp: 4 (over y, core).
Axes of the slice: x: 2, y: 2, z: 4, core: 2. Of those that a mesh axis runs over, the one named last changes fastest.
Arguments:
- embeddings: bfloat16 [128, 56, 1536], P('dp'), may hold values from -6 to 6
- samples: int32 [128, 56, 32], P('dp'), may hold values from 0 to 31
- seq_lengths: int32 [128], P('dp'), may hold values from 10 to 56, as said below
- gru_weight: float32 [3, 2048, 1024], P(None, None, 'tp'), may hold values from -0.375 to 0.375
- post_weight: float32 [2560, 1024], P(None, 'tp'), may hold values from -0.25 to 0.25
- prior_weight: float32 [1024, 1024], P(None, 'tp'), may hold values from -0.75 to 0.75
- gru_moment: float32 [3, 2048, 1024], P(None, None, 'tp'), may hold values from -0.009765625 to 0.009765625
- post_moment: float32 [2560, 1024], P(None, 'tp'), may hold values from -0.009765625 to 0.009765625
- prior_moment: float32 [1024, 1024], P(None, 'tp'), may hold values from -0.009765625 to 0.009765625
Outputs:
- loss_value: float32 [], replicated
- embed_grad: float32 [128, 56, 1536], P('dp', None, 'tp')
- new_gru: float32 [3, 2048, 1024], P(None, 'dp', 'tp')
- new_post: float32 [2560, 1024], P('dp', 'tp')
- new_prior: float32 [1024, 1024], P('dp', 'tp')
- new_gru_moment: float32 [3, 2048, 1024], P(None, 'dp', 'tp')
- new_post_moment: float32 [2560, 1024], P('dp', 'tp')
- new_prior_moment: float32 [1024, 1024], P('dp', 'tp')
Inputs may be any that keep to these rules, and one draw needn't show every extreme that they name: `seq_lengths`: the frames of a sequence at positions below its count are true frames, the rest are padding; the sequences of every index of dp include one with exactly 56, and some sequence has exactly 56 // 6 + 1.
All inputs are finite; a program needn't handle non-finite values.
Results may differ from a plain program's by a relative error of at most 0.025.
Values may be sent and summed in bfloat16 or wider, within the bound.
No kernel may reach another device: no remote copies, remote signals or barrier semaphores. Data moves between devices by JAX's collectives and lax.ppermute only.
A program may use at most 192 MiB of HBM per device.

v0:
```python
import functools
import math

import jax
import jax.numpy as jnp
from jax import lax
from jax.experimental import pallas as pl
from jax.experimental.pallas import tpu as pltpu
from jax.sharding import PartitionSpec as P

H = 1024
ZC = 32
E = 1536
FRAMES = 56
MATS = 5
Z = 1024
ROWS = (Z + H, Z + H, Z + H, H + E, H)
PACK = 8
CHUNK = 4


coeff_linear = 3.4445
coeff_cubic = -4.775
coeff_quintic = 2.0315
momentum_keep = 0.95
learn_rate = 0.2
weight_decay = 0.01
update_scale = 0.2
tiny_value = 1e-07
mib = 1 << 20
LARGE = 56 * mib
f32 = jnp.float32
bf16 = jnp.bfloat16
NT = (((1,), (1,)), ((), ()))
TN = (((0,), (0,)), ((), ()))


def dot(left, right):
    return jnp.dot(left, right, preferred_element_type=f32)


def dot_tn(left, right):
    return lax.dot_general(left, right, TN, preferred_element_type=f32)


def dot_nt(left, right):
    return lax.dot_general(left, right, NT, preferred_element_type=f32)


def copy(source, target, semaphore):
    return pltpu.make_async_copy(source, target, semaphore)


def scan_forward(
    seqs, chunk, spot_ref, x_ref, *refs
):
    parts, packs = x_ref.shape[:2]
    shards = refs[:parts]
    h_ref, k_hbm, u_hbm, t_hbm, state, w, k_ref, u_ref, t, w_sem, k_sem, u_sem, t_sem = refs[parts:]
    units = w.shape[3]
    per_pack = PACK // seqs
    loads = [copy(shards[n], w.at[spot_ref[0] ^ n], w_sem.at[n]) for n in range(parts)]
    for load in loads:
        load.start()
    state[...] = jnp.zeros_like(state)
    for load in loads:
        load.wait()

    def stores(c):
        at = pl.ds(c * chunk, chunk)
        return (
            copy(k_ref.at[:, at], k_hbm.at[:, at], k_sem.at[c]),
            copy(u_ref.at[at], u_hbm.at[at], u_sem.at[c]),
        )

    def pack(i, carry):
        states = []
        for frame in range(per_pack):
            rows = slice(frame * seqs, (frame + 1) * seqs)
            if frame == 0:
                source, live = jnp.maximum(i - 1, 0), jnp.where(i > 0, 1.0, 0.0)
                spot = slice((per_pack - 1) * seqs, per_pack * seqs)
            else:
                source, live = i, None
                spot = slice((frame - 1) * seqs, frame * seqs)
            before = state[...]
            low = before.astype(bf16)
            news = []
            for p in range(parts):
                cols = slice(p * units, (p + 1) * units)
                given = x_ref[p, source].astype(f32)[spot]
                if live is not None:
                    given = given * live
                pre = [
                    given[:, k * units : (k + 1) * units] + dot(low, w[p, k]) for k in range(3)
                ]
                last = before[:, cols]
                r = jax.nn.sigmoid(pre[0])
                c = jnp.tanh(r * pre[1])
                u = jax.nn.sigmoid(pre[2] - 1.0)
                rest = 1.0 - u
                new = u * c + rest * last
                inner = u * (1.0 - c * c)
                state[:, cols] = new
                news.append(new)
                k_ref[0, i, rows, cols] = inner * pre[1] * r * (1.0 - r)
                k_ref[1, i, rows, cols] = inner * r
                k_ref[2, i, rows, cols] = (c - last) * u * rest
                u_ref[i, rows, cols] = rest
            states.append(jnp.concatenate(news, axis=1))
        h_ref[i] = jnp.concatenate(states, axis=0).astype(bf16)

        @pl.when(i % chunk == chunk - 1)
        def _():
            for store in stores(i // chunk):
                store.start()

        return carry

    def pack_and_turn(i, carry):
        t[pl.ds(pl.multiple_of(i * units, units), units), :] = w[i // 3, i % 3].T
        return pack(i, carry)

    lax.fori_loop(0, 3 * parts, pack_and_turn, 0)
    turned = copy(t, t_hbm, t_sem)
    turned.start()
    lax.fori_loop(3 * parts, packs, pack, 0)
    turned.wait()
    for c in range(packs // chunk):
        for store in stores(c):
            store.wait()


def scan_backward(
    seqs, chunk, d_ref, k_hbm, u_hbm, t_hbm, b_hbm, now, kept, w, k_ref, u_ref, b_ref, t_sem, k_sem, u_sem, b_sem
):
    copies, parts, packs = b_hbm.shape[:3]
    units = b_ref.shape[3] // 3
    per_pack = PACK // seqs
    chunks = packs // chunk

    def loads(c):
        at = pl.ds(c * chunk, chunk)
        return (
            copy(k_hbm.at[:, at], k_ref.at[:, at], k_sem.at[c]),
            copy(u_hbm.at[at], u_ref.at[at], u_sem.at[c]),
        )

    def stores(c):
        at = pl.ds(c * chunk, chunk)
        return [
            copy(b_ref.at[:, at], b_hbm.at[n, :, at], b_sem.at[n * chunks + c]) for n in range(copies)
        ]

    turned = copy(t_hbm, w, t_sem)
    turned.start()
    for c in reversed(range(chunks)):
        for load in loads(c):
            load.start()
    now[...] = jnp.zeros_like(now)
    kept[...] = jnp.zeros_like(kept)
    turned.wait()

    def pack(n, carry):
        i = packs - 1 - n

        @pl.when(i % chunk == chunk - 1)
        def _():
            for load in loads(i // chunk):
                load.wait()

        later = [None] * per_pack
        for frame in reversed(range(per_pack)):
            rows = slice(frame * seqs, (frame + 1) * seqs)
            values = now[...]
            later[frame] = values
            dh = d_ref[i, rows] + kept[...] + dot(values.astype(bf16), w[...])
            kept[...] = dh * u_ref[i, rows]
            for p in range(parts):
                cols = slice(p * units, (p + 1) * units)
                for k in range(3):
                    spot = slice((3 * p + k) * units, (3 * p + k + 1) * units)
                    now[:, spot] = dh[:, cols] * k_ref[k, i, rows, cols]
        stacked = jnp.concatenate(later, axis=0).astype(bf16)
        for p in range(parts):
            b_ref[p, i] = stacked[:, p * 3 * units : (p + 1) * 3 * units]

        @pl.when(i % chunk == 0)
        def _():
            for store in stores(i // chunk):
                store.start()

        return carry

    lax.fori_loop(0, packs, pack, 0)
    for c in range(chunks):
        for store in stores(c):
            store.wait()


def head_block(h_ref, e_ref, t_ref, m_ref, r_ref, w_hbm, back_ref, d_ref, loss_ref, w_ref, w_sem):
    parts = w_ref.shape[0]
    loads = [copy(w_hbm.at[p], w_ref.at[p], w_sem.at[p]) for p in range(parts)]
    for load in loads:
        load.start()
    units = w_ref.shape[2]
    rows = h_ref.shape[0]
    low = h_ref[...]
    back_ref[0] = low
    mask = m_ref[...]
    given = jnp.zeros((rows, 128), f32)
    normal = jnp.zeros((1, rows), f32)
    for p in range(parts):
        loads[p].wait()
        post = dot(low, w_ref[p, :H]) + dot(e_ref[...], w_ref[p, H : H + E])
        prior = dot(low, w_ref[p, H + E :])
        for head, logits in enumerate((prior, post)):
            for piece in range(units // 128):
                l = logits[:, piece * 128 : (piece + 1) * 128]
                cols = slice(p * units + piece * 128, p * units + (piece + 1) * 128)
                target = t_ref[:, cols].astype(f32)
                turned = l.T.reshape(128 // ZC, ZC, rows)
                top = jnp.max(turned, axis=1, keepdims=True)
                e = jnp.exp(turned - top)
                total = jnp.sum(e, axis=1, keepdims=True)
                normal = normal + jnp.sum(top + jnp.log(total), axis=0)
                probs = (e * (1.0 / total)).reshape(128, rows).T
                given = given + target * l
                back_ref[head + 2, :, cols] = (mask * (probs - target)).astype(bf16)
    loss_ref[...] = jnp.sum(r_ref[...] * normal, axis=1, keepdims=True) - jnp.sum(
        jnp.sum(mask * given, axis=0, keepdims=True), axis=1, keepdims=True
    )
    direct = jnp.zeros((rows, H), f32)
    for p in range(parts):
        cols = slice(p * units, (p + 1) * units)
        direct = direct + dot_nt(back_ref[2, :, cols], w_ref[p, H + E :])
        direct = direct + dot_nt(back_ref[3, :, cols], w_ref[p, :H])
    d_ref[...] = direct


def head_grads(spot_ref, scale_ref, r_hbm, e_hbm, earlier_ref, o_ref, h_ref, r_ref, e_ref, sems):
    parts, rows = e_ref.shape[0], e_ref.shape[1]
    units = o_ref.shape[1]
    frames = parts * rows
    scale = scale_ref[0]
    own = pl.ds(pl.multiple_of(spot_ref[0] * units, units), units)
    loads = [
        copy(r_hbm.at[:, pl.ds(2, 2), :, own], r_ref, sems.at[0]),
        copy(r_hbm.at[:, 0], h_ref, sems.at[1]),
        copy(e_hbm, e_ref, sems.at[2]),
    ]
    for load in loads:
        load.start()
    loads[0].wait()
    loads[1].wait()
    post = r_ref[:, 1].reshape(frames, units)
    both = jnp.concatenate([post, r_ref[:, 0].reshape(frames, units)], axis=1)
    for m in range(H // 256):
        spot = slice(m * 256, (m + 1) * 256)
        grad = (dot_tn(h_ref[:, :, spot].reshape(frames, 256), both) * scale).astype(bf16)
        o_ref[m * 256 : (m + 1) * 256] = grad[:, :units]
        o_ref[H + E + m * 256 : H + E + (m + 1) * 256] = grad[:, units:]
    loads[2].wait()
    for m in range(E // 256):
        spot = slice(m * 256, (m + 1) * 256)
        grad = (dot_tn(e_ref[:, :, spot].reshape(frames, 256), post) * scale).astype(bf16)
        o_ref[H + m * 256 : H + (m + 1) * 256] = grad


def gru_grads(
    spot_ref, scale_ref, one_hbm, r_hbm, b_hbm, earlier_ref, o_ref, one_ref, l_ref, b_ref, sems
):
    parts, rows = b_ref.shape[1], b_ref.shape[2]
    units = o_ref.shape[2]
    frames = parts * rows
    share = o_ref.shape[1] // 3
    half = o_ref.shape[0] // 2
    scale = scale_ref[0]
    me = spot_ref[1]
    loads = [copy(b_hbm, b_ref, sems.at[0]), copy(one_hbm, one_ref, sems.at[1])]
    for z in range(half):
        spot = pl.ds(pl.multiple_of((z * 2 + me) * share, share), share)
        loads.append(copy(r_hbm.at[:, 0, :, spot], l_ref.at[0, z], sems.at[2 + 2 * z]))
        loads.append(copy(r_hbm.at[:, 1, :, spot], l_ref.at[1, z], sems.at[3 + 2 * z]))
    for load in loads:
        load.start()
    loads[0].wait()
    loads[1].wait()
    back = [b_ref[x].reshape(frames, 3 * units) for x in (me, 1 - me)]
    for z in range(2 * half):
        if z < half:
            spot = slice(z * share, (z + 1) * share)
            left = [one_ref[x, :, spot] for x in (me, 1 - me)]
        else:
            loads[2 * (z - half) + 2].wait()
            loads[2 * (z - half) + 3].wait()
            left = [l_ref[n, z - half].reshape(frames, share) for n in (0, 1)]
        grad = (dot_tn(left[0], back[0]) + dot_tn(left[1], back[1])) * scale
        grad = grad.astype(bf16)
        for k in range(3):
            o_ref[z, k * share : (k + 1) * share] = grad[:, k * units : (k + 1) * units]


def orthogonal_block(base, tile, own_ref, g_ref, *refs):
    o_ref, x, a, b = refs[-4:]
    side, width = g_ref.shape
    share = o_ref.shape[0]
    own = pl.ds(pl.multiple_of(own_ref[0] * share, share), share)
    wide = own_ref[1] > 0

    def either(run):
        pl.when(wide)(functools.partial(run, width))
        pl.when(jnp.logical_not(wide))(functools.partial(run, base))

    def squares(i, total):
        rows = pl.ds(pl.multiple_of(i * 128, 128), 128)
        v = g_ref[rows, :].astype(f32)
        return total + jnp.sum(v * v)

    total = lax.fori_loop(0, side // 128, squares, jnp.zeros((), f32))
    scale = 1.0 / (jnp.sqrt(jnp.full((1, 128), total, f32)) + tiny_value)
    scale = scale[:, :1]

    def shrink(i, carry):
        rows = pl.ds(pl.multiple_of(i * 128, 128), 128)
        x[rows, :] = (g_ref[rows, :].astype(f32) * scale).astype(bf16)
        return carry

    lax.fori_loop(0, side // 128, shrink, 0)

    def lower(out, product):
        for start in range(0, side, 256):
            stop = start + 256
            block = product(slice(start, side), slice(start, stop)).astype(bf16)
            out[start:, start:stop] = block
            if stop < side:
                out[start:stop, stop:] = block[256:].T

    def square(depth):
        lower(a, lambda rows, cols: dot_nt(x[rows, :depth], x[cols, :depth]))

    def mix():
        lower(
            b,
            lambda rows, cols: coeff_cubic * a[rows, cols].astype(f32)
            + coeff_quintic * dot(a[rows, :], a[:, cols]),
        )

    def renew_all(depth):
        for start in range(0, depth, tile):
            cols = slice(start, start + tile)
            x[:, cols] = (
                coeff_linear * x[:, cols].astype(f32) + dot(b[...], x[:, cols])
            ).astype(bf16)

    def sweep(s, carry):
        either(square)
        mix()
        either(renew_all)
        return carry

    lax.fori_loop(0, 4, sweep, 0)
    either(square)
    part = (coeff_cubic * a[own, :].astype(f32) + coeff_quintic * dot(a[own, :], a[...])).astype(bf16)

    def last(j, carry):
        cols = pl.ds(pl.multiple_of(j * tile, tile), tile)
        o_ref[:, cols] = (
            coeff_linear * x[own, cols].astype(f32) + dot(part, x[:, cols])
        ).astype(bf16)
        return carry

    lax.fori_loop(0, width // tile, last, 0)


def turn_block(tile, g_ref, o_ref):
    def block(i, carry):
        spot = pl.ds(pl.multiple_of(i * tile, tile), tile)
        o_ref[:, spot] = g_ref[spot, :].T
        return carry

    lax.fori_loop(0, g_ref.shape[0] // tile, block, 0)


def collect_block(base, spot_ref, *refs):
    *pieces, o_ref, rows = refs
    steps = len(pieces)
    more = pieces[0].shape[0] - base
    for step, piece in enumerate(pieces):
        d = spot_ref[0] ^ step
        o_ref[:, pl.ds(pl.multiple_of(d * base, base), base)] = piece[:base].T
        rows[pl.ds(pl.multiple_of(d * more, more), more), :] = piece[base:]
    o_ref[:, steps * base :] = rows[...].T


def deal_block(base, spot_ref, g_ref, o_ref, rows):
    steps, widest = o_ref.shape[:2]
    more = widest - base
    rows[...] = g_ref[:, steps * base :].T
    for step in range(steps):
        d = spot_ref[0] ^ step
        o_ref[step, :base] = g_ref[:, pl.ds(pl.multiple_of(d * base, base), base)].T
        o_ref[step, base:] = rows[pl.ds(pl.multiple_of(d * more, more), more), :]


def finish_block(owners, spot_ref, *refs):
    pieces, (gru_ref, post_ref, prior_ref), (gru_out, post_out, prior_out), all_ref = (
        refs[:-7],
        refs[-7:-4],
        refs[-4:-1],
        refs[-1],
    )
    for step, piece in enumerate(pieces):
        all_ref[step] = piece[...]

    def renewed(old, m):
        change = all_ref[spot_ref[0] ^ owners[m], : old.shape[0]].astype(f32)
        factor = learn_rate * update_scale * math.sqrt(max(ROWS[m], Z))
        return old * (1.0 - learn_rate * weight_decay) - factor * change

    for k in range(3):
        gru_out[k] = renewed(gru_ref[k], k)
    post_out[...] = renewed(post_ref[...], 3)
    prior_out[...] = renewed(prior_ref[...], 4)


def in_vmem(count):
    return [pl.BlockSpec(memory_space=pltpu.VMEM)] * count


def cost(flops, touched):
    return pl.CostEstimate(flops=int(flops), bytes_accessed=int(touched), transcendentals=0)


def run_forward(spot, inputs, weights, seqs):
    parts, packs = inputs.shape[:2]
    units = weights[0].shape[2]
    chunks = packs // CHUNK
    return pl.pallas_call(
        functools.partial(scan_forward, seqs, CHUNK),
        out_shape=[
            jax.ShapeDtypeStruct((packs, PACK, H), bf16),
            jax.ShapeDtypeStruct((3, packs, PACK, H), f32),
            jax.ShapeDtypeStruct((packs, PACK, H), f32),
            jax.ShapeDtypeStruct((3 * H, H), bf16),
        ],
        in_specs=in_smem(1) + in_vmem(1) + anywhere(parts),
        out_specs=in_vmem(1) + anywhere(3),
        scratch_shapes=[
            pltpu.VMEM((seqs, H), f32),
            pltpu.VMEM((parts, 3, H, units), bf16),
            pltpu.VMEM((3, packs, PACK, H), f32),
            pltpu.VMEM((packs, PACK, H), f32),
            pltpu.VMEM((3 * H, H), bf16),
            pltpu.SemaphoreType.DMA((parts,)),
            pltpu.SemaphoreType.DMA((chunks,)),
            pltpu.SemaphoreType.DMA((chunks,)),
            pltpu.SemaphoreType.DMA,
        ],
        compiler_params=pltpu.CompilerParams(vmem_limit_bytes=LARGE),
        cost_estimate=cost(6e10, 20 * mib),
        name="scan_forward",
    )(spot, inputs, *weights)


def run_backward(direct, factors, rest, turned, parts, seqs, copies):
    packs = direct.shape[0]
    units = H // parts
    chunks = packs // CHUNK
    return pl.pallas_call(
        functools.partial(scan_backward, seqs, CHUNK),
        out_shape=jax.ShapeDtypeStruct((copies, parts, packs, PACK, 3 * units), bf16),
        in_specs=in_vmem(1) + anywhere(3),
        out_specs=anywhere(1)[0],
        scratch_shapes=[
            pltpu.VMEM((seqs, 3 * H), f32),
            pltpu.VMEM((seqs, H), f32),
            pltpu.VMEM((3 * H, H), bf16),
            pltpu.VMEM((3, packs, PACK, H), f32),
            pltpu.VMEM((packs, PACK, H), f32),
            pltpu.VMEM((parts, packs, PACK, 3 * units), bf16),
            pltpu.SemaphoreType.DMA,
            pltpu.SemaphoreType.DMA((chunks,)),
            pltpu.SemaphoreType.DMA((chunks,)),
            pltpu.SemaphoreType.DMA((copies * chunks,)),
        ],
        compiler_params=pltpu.CompilerParams(vmem_limit_bytes=LARGE),
        cost_estimate=cost(6e10, 20 * mib),
        name="scan_backward",
    )(direct, factors, rest, turned)


def run_heads(hidden, embed, target, mask, mask_row, weights):
    rows = hidden.shape[0]
    return pl.pallas_call(
        head_block,
        out_shape=[
            jax.ShapeDtypeStruct((4, rows, Z), bf16),
            jax.ShapeDtypeStruct((rows, H), f32),
            jax.ShapeDtypeStruct((1, 1), f32),
        ],
        in_specs=in_vmem(5) + anywhere(1),
        out_specs=in_vmem(3),
        scratch_shapes=[
            pltpu.VMEM(weights.shape, bf16),
            pltpu.SemaphoreType.DMA((weights.shape[0],)),
        ],
        compiler_params=pltpu.CompilerParams(vmem_limit_bytes=LARGE),
        cost_estimate=cost(1e10, 12 * mib),
        name="heads",
    )(hidden, embed, target, mask, mask_row, weights)


def in_smem(count):
    return [pl.BlockSpec(memory_space=pltpu.SMEM)] * count


def anywhere(count):
    return [pl.BlockSpec(memory_space=pl.ANY)] * count


def run_head_grads(spot, scale, everyone, embed, earlier):
    parts, rows = embed.shape[:2]
    units = H // parts
    return pl.pallas_call(
        head_grads,
        out_shape=jax.ShapeDtypeStruct((H + E + H, units), bf16),
        in_specs=in_smem(2) + anywhere(3),
        out_specs=in_vmem(1)[0],
        scratch_shapes=[
            pltpu.VMEM((parts, rows, H), bf16),
            pltpu.VMEM((parts, 2, rows, units), bf16),
            pltpu.VMEM(embed.shape, bf16),
            pltpu.SemaphoreType.DMA((3,)),
        ],
        compiler_params=pltpu.CompilerParams(vmem_limit_bytes=LARGE),
        cost_estimate=cost(4e9, 12 * mib),
        name="head_grads",
    )(spot, scale, everyone, embed, earlier)


def run_gru_grads(spot, scale, onehot, everyone, back, earlier, dz_count):
    parts, rows = back.shape[1:3]
    units = back.shape[3] // 3
    share = (Z + H) // (2 * dz_count)
    return pl.pallas_call(
        gru_grads,
        out_shape=jax.ShapeDtypeStruct((dz_count, 3 * share, units), bf16),
        in_specs=in_smem(2) + anywhere(4),
        out_specs=in_vmem(1)[0],
        scratch_shapes=[
            pltpu.VMEM(onehot.shape, bf16),
            pltpu.VMEM((2, dz_count // 2, parts, rows, share), bf16),
            pltpu.VMEM(back.shape, bf16),
            pltpu.SemaphoreType.DMA((2 + dz_count,)),
        ],
        compiler_params=pltpu.CompilerParams(vmem_limit_bytes=LARGE),
        cost_estimate=cost(4e9, 12 * mib),
        name="gru_grads",
    )(spot, scale, onehot, everyone, back, earlier)


def plain_gru_grads(dx_index, scale, onehot, everyone, back, dz_count):
    units = back.shape[3] // 3
    share = (Z + H) // (2 * dz_count)
    total = 0.0
    for states, x in ((everyone[:, 0], dx_index), (everyone[:, 1], 1 - dx_index)):
        states = states.reshape(-1, dz_count // 2, 2, share)
        states = lax.dynamic_index_in_dim(states, dx_index, 2, keepdims=False)
        ones = lax.dynamic_index_in_dim(onehot, x, 0, keepdims=False)
        left = jnp.concatenate([ones, states.reshape(ones.shape)], axis=1)
        right = lax.dynamic_index_in_dim(back, x, 0, keepdims=False)
        total = total + dot_tn(left, right.reshape(-1, 3 * units))
    grads = (total * scale).astype(bf16).reshape(dz_count, share, 3, units)
    return jnp.swapaxes(grads, 1, 2).reshape(dz_count, 3 * share, units)


def run_orthogonal(base, share, own, matrix, earlier):
    side, width = matrix.shape
    return pl.pallas_call(
        functools.partial(orthogonal_block, base, 512),
        out_shape=jax.ShapeDtypeStruct((share, width), bf16),
        in_specs=in_smem(1) + in_vmem(1) + anywhere(len(earlier)),
        out_specs=in_vmem(1)[0],
        scratch_shapes=[
            pltpu.VMEM((side, width), bf16),
            pltpu.VMEM((side, side), bf16),
            pltpu.VMEM((side, side), bf16),
        ],
        compiler_params=pltpu.CompilerParams(vmem_limit_bytes=28 * mib),
        cost_estimate=cost(5e10, 6 * mib),
        name="orthogonal",
    )(own, matrix, *earlier)


def run_turn(matrix):
    return pl.pallas_call(
        functools.partial(turn_block, 256),
        out_shape=jax.ShapeDtypeStruct(matrix.shape[::-1], bf16),
        in_specs=in_vmem(1),
        out_specs=in_vmem(1)[0],
        compiler_params=pltpu.CompilerParams(vmem_limit_bytes=6 * mib),
        cost_estimate=cost(1e6, 3 * mib),
        name="turn",
    )(matrix)


def small_kernel(body, out_shape, scratch, specs, arguments, name):
    return pl.pallas_call(
        body,
        out_shape=out_shape,
        in_specs=specs,
        out_specs=jax.tree.map(lambda _: in_vmem(1)[0], out_shape),
        scratch_shapes=scratch,
        compiler_params=pltpu.CompilerParams(vmem_limit_bytes=8 * mib),
        cost_estimate=cost(1e6, 4 * mib),
        name=name,
    )(*arguments)


def run_collect(spot, pieces, base):
    steps = len(pieces)
    widest, units = pieces[0].shape
    return small_kernel(
        functools.partial(collect_block, base),
        jax.ShapeDtypeStruct((units, steps * widest), bf16),
        [pltpu.VMEM((steps * (widest - base), units), bf16)],
        in_smem(1) + in_vmem(steps),
        (spot, *pieces),
        "collect",
    )


def run_deal(spot, result, steps, base):
    units, width = result.shape
    widest = width // steps
    return small_kernel(
        functools.partial(deal_block, base),
        jax.ShapeDtypeStruct((steps, widest, units), bf16),
        [pltpu.VMEM((steps * (widest - base), units), bf16)],
        in_smem(1) + in_vmem(1),
        (spot, result),
        "deal",
    )


def run_finish(owners, spot, pieces, rows):
    return small_kernel(
        functools.partial(finish_block, owners),
        [jax.ShapeDtypeStruct(block.shape, f32) for block in rows],
        [pltpu.VMEM((len(pieces), *pieces[0].shape), bf16)],
        in_smem(1) + in_vmem(len(pieces) + len(rows)),
        (spot, *pieces, *rows),
        "finish",
    )


def on_device(
    embeddings,
    samples,
    seq_lengths,
    gru_weight,
    post_weight,
    prior_weight,
    gru_moment,
    post_moment,
    prior_moment,
):
    dz_count = lax.axis_size("dz")
    dx_count = lax.axis_size("dx")
    tp_count = lax.axis_size("tp")
    dp_count = dz_count * dx_count
    dx_index = lax.axis_index("dx")
    tp_index = lax.axis_index("tp")
    dp_index = lax.axis_index("dz") * dx_count + dx_index
    seq_count = embeddings.shape[0]
    seqs = seq_count // tp_count
    units = gru_weight.shape[2]
    groups = Z // ZC
    rows = seqs * FRAMES
    packs = rows // PACK

    def gather(block):
        return lax.all_gather(block, "tp", axis=0, tiled=False)

    def exchange(block, axis):
        return lax.all_to_all(block, axis, 0, 0, tiled=True)

    def mine(block, axis):
        return lax.dynamic_index_in_dim(block, dx_index, axis, keepdims=False)

    def across(block, bit):
        return lax.ppermute(block, "tp", [(i, i ^ bit) for i in range(tp_count)])

    own_hidden = gru_weight[:, Z:].astype(bf16)
    far = across(own_hidden, 2)
    near = across(own_hidden, 1)
    gru_input = lax.optimization_barrier(gru_weight)
    head_low = jnp.concatenate([post_weight.astype(bf16), prior_weight.astype(bf16)], axis=0)

    by_part = jnp.swapaxes(samples.reshape(tp_count, seqs, FRAMES, groups), 1, 2)
    by_part = by_part.reshape(tp_count * rows, groups).astype(bf16)

    def one_hot(chosen):
        count = chosen.shape[-1]
        classes = jnp.arange(count * ZC, dtype=jnp.int32)
        expand = (classes[None, :] // ZC == jnp.arange(count)[:, None]).astype(bf16)
        return (dot(chosen, expand) == (classes % ZC).astype(f32)).astype(bf16)

    onehot = one_hot(by_part)
    input_part = jnp.concatenate(
        [dot(onehot, gru_input[k, :Z].astype(bf16)).astype(bf16) for k in range(3)], axis=1
    ).reshape(tp_count, packs, PACK, 3 * units)
    input_part = exchange(input_part, "tp")
    embed_rows = jnp.swapaxes(embeddings.reshape(tp_count, seqs, FRAMES, E), 1, 2)
    embed_rows = embed_rows.reshape(tp_count, rows, E)
    pair_samples = lax.all_gather(by_part, "dx", axis=0, tiled=False)
    half = Z // dx_count
    pair_half = mine(
        pair_samples.reshape(dx_count * tp_count * rows, dz_count // 2, dx_count, -1), 2
    )
    pair_onehot = one_hot(pair_half.reshape(dx_count * tp_count * rows, groups // dx_count))
    pair_onehot = pair_onehot.reshape(dx_count, tp_count * rows, half)
    own_embed = lax.dynamic_index_in_dim(embed_rows, tp_index, 0, keepdims=False)
    onehot = onehot.reshape(tp_count, rows, Z)
    own_target = lax.dynamic_index_in_dim(onehot, tp_index, 0, keepdims=False)
    positions = jnp.arange(FRAMES, dtype=jnp.int32)
    own_lengths = lax.dynamic_slice_in_dim(seq_lengths, tp_index * seqs, seqs, 0)
    frame_mask = (positions[:, None] < own_lengths[None, :]).astype(f32)
    mask_lanes = jnp.broadcast_to(frame_mask.reshape(rows, 1), (rows, 128))

    weights = [own_hidden, near, far, across(far, 1)]
    every_mask = (positions[:, None] < seq_lengths[None, :]).astype(f32)
    frame_count = jnp.broadcast_to(jnp.sum(every_mask), (8, 128))
    for axis, bits in (("dx", dx_count), ("dz", dz_count)):
        for bit in range(bits.bit_length() - 1):
            pairs = [(i, i ^ (1 << bit)) for i in range(bits)]
            frame_count = frame_count + lax.ppermute(frame_count, axis, pairs)
    frame_count = frame_count[0, 0]
    scale = (1.0 / frame_count).reshape(1)

    early = (head_low, own_embed, own_target, mask_lanes, embed_rows, pair_onehot, scale)
    weights, input_part, early = lax.optimization_barrier((weights, input_part, early))
    head_low, own_embed, own_target, mask_lanes, embed_rows, pair_onehot, scale = early
    head_full = gather(head_low)
    hidden, factors, rest, turned = run_forward(tp_index.astype(jnp.int32).reshape(1), input_part, weights, seqs)
    hidden = hidden.reshape(rows, H)
    swap = [(i, i ^ 1) for i in range(dx_count)]
    neighbour = lax.ppermute(hidden, "dx", swap)
    backs, direct, loss_lanes = run_heads(
        hidden, own_embed, own_target, mask_lanes, frame_mask.reshape(1, rows), head_full
    )
    everyone = gather(lax.dynamic_update_slice(backs, neighbour[None], (1, 0, 0)))
    back = run_backward(
        direct.reshape(packs, PACK, H), factors, rest, turned, tp_count, seqs, dx_count
    )
    own_back = exchange(back.reshape(dx_count * tp_count, rows, 3 * units), ("dx", "tp"))
    own_back = own_back.reshape(dx_count, tp_count, rows, 3 * units)

    shares = [size // dp_count for size in ROWS]
    all_post = everyone[:, 3]
    spot = jnp.stack([tp_index, dx_index]).astype(jnp.int32)

    head_grad = run_head_grads(spot, scale, everyone, embed_rows, back)
    own_back, _ = lax.optimization_barrier((own_back, head_grad))

    head_grad = jnp.concatenate(
        [
            block.reshape(dz_count, dx_count, -1, units)
            for block in (head_grad[: H + E], head_grad[H + E :])
        ],
        axis=2,
    )

    def share_rows(block):
        return lax.psum_scatter(block, "dz", scatter_dimension=0, tiled=True)[0]

    head_done = share_rows(head_grad)
    if shares[0] % 128 == 0:
        gru_grad = run_gru_grads(
            spot, scale, pair_onehot, everyone, own_back, head_grad, dz_count
        )
    else:
        gru_grad = plain_gru_grads(dx_index, scale, pair_onehot, everyone, own_back, dz_count)
    gru_grad, head_done = lax.optimization_barrier((gru_grad, head_done))
    gru_sum = share_rows(gru_grad).astype(f32)
    received = lax.ppermute(
        lax.dynamic_index_in_dim(head_done, 1 - dx_index, 0, keepdims=False), "dx", swap
    )
    head_sum = mine(head_done, 0).astype(f32) + received.astype(f32)
    loss_sum = jnp.broadcast_to(jnp.sum(loss_lanes), (8, 128))
    for axis, bits in (("tp", tp_count), ("dx", dx_count), ("dz", dz_count)):
        for bit in range(bits.bit_length() - 1):
            pairs = [(i, i ^ (1 << bit)) for i in range(bits)]
            loss_sum = loss_sum + lax.ppermute(loss_sum, axis, pairs)
    loss_sum = loss_sum[0, 0]
    loss_value = loss_sum / frame_count

    embed_part = E // tp_count
    own_rows_e = lax.dynamic_slice_in_dim(head_full, H + tp_index * embed_part, embed_part, 1)
    post_by_seq = jnp.swapaxes(all_post.reshape(tp_count, FRAMES, seqs, Z), 1, 2)
    embed_grad = jnp.einsum(
        "psfk,ek->psfe",
        post_by_seq,
        jnp.concatenate(list(own_rows_e), axis=1),
        preferred_element_type=f32,
    ).reshape(seq_count, FRAMES, embed_part)
    embed_grad = embed_grad * scale[0]

    grads = [gru_sum[k * shares[0] : (k + 1) * shares[0]] for k in range(3)]
    grads += [head_sum[: shares[3]], head_sum[shares[3] :]]

    def own_rows(matrix, axis_dim):
        share = matrix.shape[axis_dim] // dp_count
        return lax.dynamic_slice_in_dim(matrix, dp_index * share, share, axis_dim)

    gru_moments = own_rows(gru_moment, 1)
    moments = [momentum_keep * gru_moments[k] + grads[k] for k in range(3)]
    moments.append(momentum_keep * own_rows(post_moment, 0) + grads[3])
    moments.append(momentum_keep * own_rows(prior_moment, 0) + grads[4])
    ahead = [(grads[m] + momentum_keep * moments[m]).astype(bf16) for m in range(MATS)]

    owners = [m * dp_count // 8 for m in (0, 3, 4, 7, 5)]
    widest = max(shares)
    base = shares[0]
    holds_post = (dp_index == owners[3]).astype(jnp.int32)
    if dp_count == 8:
        kept = jnp.array([owners.index(d) if d in owners else 0 for d in range(dp_count)])
        blocks = jnp.stack(
            [jnp.pad(block, ((0, widest - block.shape[0]), (0, 0))) for block in ahead]
        )
        where = dp_index.astype(jnp.int32).reshape(1)
        pieces = []
        for step in range(dp_count):
            block = lax.dynamic_index_in_dim(blocks, kept[dp_index ^ step], 0, keepdims=False)
            if step > 0:
                block = lax.ppermute(block, ("dz", "dx"), [(d ^ step, d) for d in owners])
            pieces.append(block)
        turned = run_collect(where, pieces, base)
    else:
        slots = [jnp.zeros((widest, units), bf16)] * dp_count
        for m in range(MATS):
            slots[owners[m]] = jnp.pad(ahead[m], ((0, widest - shares[m]), (0, 0)))
        arrived = exchange(jnp.stack(slots), ("dz", "dx"))
        turned = run_turn(
            jnp.concatenate(
                [arrived[:, :base].reshape(-1, units), arrived[:, base:].reshape(-1, units)], axis=0
            )
        )
    wide = gather(turned).reshape(H, dp_count * widest)
    own = jnp.stack([tp_index, holds_post]).astype(jnp.int32)
    old_rows = (own_rows(gru_weight, 1), own_rows(post_weight, 0), own_rows(prior_weight, 0))
    old_rows = lax.optimization_barrier(old_rows)
    result = run_orthogonal(
        dp_count * base, units, own, wide, (embed_grad, loss_value.reshape(1, 1), *old_rows)
    )
    if dp_count == 8:
        dealt = run_deal(where, result, dp_count, base)
        pieces = [dealt[0]]
        for step in range(1, dp_count):
            pairs = [(d, d ^ step) for d in owners]
            pieces.append(lax.ppermute(dealt[step], ("dz", "dx"), pairs))
        new_gru, new_post, new_prior = run_finish(owners, where, pieces, old_rows)
    else:
        result = result.T
        results = exchange(
            jnp.concatenate(
                [
                    result[: dp_count * base].reshape(dp_count, base, units),
                    result[dp_count * base :].reshape(dp_count, widest - base, units),
                ],
                axis=1,
            ),
            ("dz", "dx"),
        )

        def renew(old, m):
            factor = learn_rate * update_scale * math.sqrt(max(ROWS[m], Z))
            change = results[owners[m], : old.shape[0]].astype(f32)
            return old * (1.0 - learn_rate * weight_decay) - factor * change

        new_gru = jnp.stack([renew(old_rows[0][k], k) for k in range(3)])
        new_post = renew(old_rows[1], 3)
        new_prior = renew(old_rows[2], 4)
    return (
        loss_value,
        embed_grad,
        new_gru,
        new_post,
        new_prior,
        jnp.stack(moments[:3]),
        moments[3],
        moments[4],
    )

def solution(mesh):
    dp_count, tp_count = mesh.devices.shape
    mesh = jax.sharding.Mesh(
        mesh.devices.reshape(dp_count // 2, 2, tp_count), ("dz", "dx", "tp")
    )
    dp = ("dz", "dx")
    in_specs = (
        P(dp, None, None),
        P(dp, None, None),
        P(dp),
        P(None, None, "tp"),
        P(None, "tp"),
        P(None, "tp"),
        P(None, None, "tp"),
        P(None, "tp"),
        P(None, "tp"),
    )
    out_specs = (
        P(),
        P(dp, None, "tp"),
        P(None, dp, "tp"),
        P(dp, "tp"),
        P(dp, "tp"),
        P(None, dp, "tp"),
        P(dp, "tp"),
        P(dp, "tp"),
    )
    return jax.shard_map(
        on_device, mesh=mesh, in_specs=in_specs, out_specs=out_specs, check_vma=False
    )
```

profile of v0, /device:TPU:9, one launch (start us, length us, event | category | flops | bytes accessed | tf_op | source)
XLA Modules:
  0.0 477.2 jit_solution(6309404700272953319)
XLA Ops:
  7.2 3.3 slice.186.refs_0_
  10.5 1.2 collective-permute-start.1
  12.9 3.1 convert.16
  16.0 2.2 fusion.46
  20.6 1.5 copy.39
  22.2 4.5 all-to-all-start
  28.0 1.3 collective-permute-start.3
  29.4 4.1 all_gather.24
  33.7 12.4 %collective-permute-done.1.refs_2_ = bf16[3,1024,256]{2,1,0:T(8,128)(2,1)} collective-permute-done((bf16[3,1024,256]{2,1,0:T(8,128)(2,1)}, bf16[3,1024,256]{2,1,0:T(8,128)(2,1)}, u32[]{:S(2)}, u32[]{:S(2)}) %collective-permute-start.1) | collective-permute-done | bytes 1572896 | tf_op jit(solution)/shard_map/ppermute | solution.py:693
  46.1 2.7 collective-permute-start.2
  48.8 1.9 compare_convert_fusion
  50.7 1.3 convert_element_type.145
  52.0 1.2 convert_element_type.144
  53.2 1.0 copy-done.3
  54.2 1.4 copy.53
  55.6 2.3 reshape.263.e_hbm
  57.9 2.6 pad_maximum_fusion
  60.6 2.0 dynamic-slice_bitcast_fusion.e_ref
  63.4 2.4 collective-permute-done.4
  66.5 2.4 collective-permute-start.5
  68.9 1.8 dynamic-slice_bitcast_fusion.1.t_ref
  73.8 57.2 %scan_forward.1 = (bf16[28,8,1024]{2,1,0:T(8,128)(2,1)}, f32[3,28,8,1024]{3,2,1,0:T(8,128)}, f32[28,8,1024]{2,1,0:T(8,128)}, bf16[3072,1024]{1,0:T(8,128)(2,1)}) custom-call(s32[1]{0:T(128)} %bitcast.spot_ref, bf16[4,28,8,768]{3,2,1,0:T(8,128)(2,1)} %all-to-all-done.x_ref, bf16[3,1024,256]{2,1,0:T(8,128)(2,1)} %slice.186.refs_0_, ...), custom_call_target="tpu_custom_call" | custom-call | flops 60000002048 | bytes 20971520 | tf_op jit(solution)/shard_map/scan_forward/pallas_call | solution.py:439
  131.0 1.3 collective-permute-start.11
  132.3 8.8 %heads.1 = (bf16[4,224,1024]{2,1,0:T(8,128)(2,1)}, f32[224,1024]{1,0:T(8,128)}, f32[1,1]{1,0:T(1,128)}) custom-call(bf16[224,1024]{1,0:T(8,128)(2,1)} %bitcast.215, bf16[224,1536]{1,0:T(8,128)(2,1)} %dynamic-slice_bitcast_fusion.e_ref, bf16[224,1024]{1,0:T(8,128)(2,1)} %dynamic-slice_bitcast_fusion.1.t_ref, f32[224,128]{1,0:T(8,128)} %broadcast_in_dim.6.m_ref, ...), custom_call_target="tpu_custom_call" | custom-call | flops 10000000000 | bytes 12582912 | tf_op jit(solution)/shard_map/heads/pallas_call | solution.py:495
  143.3 54.4 %scan_backward.1.earlier_ref = bf16[2,4,28,8,768]{4,3,2,1,0:T(8,128)(2,1)} custom-call(f32[28,8,1024]{2,1,0:T(8,128)} %bitcast.216, f32[3,28,8,1024]{3,2,1,0:T(8,128)} %get-tuple-element.51.k_hbm, f32[28,8,1024]{2,1,0:T(8,128)} %get-tuple-element.52.u_hbm, bf16[3072,1024]{1,0:T(8,128)(2,1)} %get-tuple-element.53.t_hbm), custom_call_target="tpu_custom_call" | custom-call | flops 60000002048 | bytes 20971520 | tf_op jit(solution)/shard_map/scan_backward/pallas_call | solution.py:470
  197.7 6.1 %head_grads.1 = bf16[3584,256]{1,0:T(8,128)(2,1)} custom-call(s32[2]{0:T(128)} %pad_add_fusion.1.spot_ref, f32[1]{0:T(128)} %bitcast.17.scale_ref, bf16[4,4,224,1024]{3,2,1,0:T(8,128)(2,1)} %all-gather.6.cloned.1.call-done.r_hbm, bf16[4,224,1536]{2,1,0:T(8,128)(2,1)} %reshape.263.e_hbm, bf16[2,4,28,8,768]{4,3,2,1,0:T(8,128)(2,1)} %scan_backward.1.earlier_ref), custom_call_target="tpu_custom_call" | custom-call | flops 4000000000 | bytes 12582912 | tf_op jit(solution)/shard_map/head_grads/pallas_call | solution.py:525
  205.3 1.4 pad_maximum_fusion.1.earlier_ref
  207.8 39.3 %all_to_all.10 = bf16[8,224,768]{2,1,0:T(8,128)(2,1)} all-to-all(bf16[8,224,768]{2,1,0:T(8,128)(2,1)S(1)} %bitcast.203), channel_id=1, replica_groups=mesh['dz'=4,'dx'=2,'tp'=4] {'dx','tp'}, dimensions={0} | all-to-all | bytes 5505024 | tf_op jit(solution)/shard_map/all_to_all | solution.py:687
  247.1 8.6 %gru_grads.1 = bf16[4,768,256]{2,1,0:T(8,128)(2,1)} custom-call(s32[2]{0:T(128)} %pad_add_fusion.1.spot_ref, f32[1]{0:T(128)} %bitcast.17.scale_ref, bf16[2,896,512]{2,1,0:T(8,128)(2,1)} %bitcast.199, bf16[4,4,224,1024]{3,2,1,0:T(8,128)(2,1)} %all-gather.6.cloned.1.call-done.r_hbm, bf16[2,4,224,768]{3,2,1,0:T(8,128)(2,1)} %bitcast.198, ...), custom_call_target="tpu_custom_call" | custom-call | flops 4000000000 | bytes 12582912 | tf_op jit(solution)/shard_map/gru_grads/pallas_call | solution.py:546
  273.1 1.6 add_convert_fusion.4
  274.7 13.6 %reduce-scatter.5.cloned.1.call-done = bf16[1,768,256]{2,1,0:T(8,128)(2,1)} async-done(((bf16[4,768,256]{2,1,0:T(8,128)(2,1)}), bf16[1,768,256]{2,1,0:T(8,128)(2,1)}) %reduce-scatter.5.cloned.1.call-update) | async-done | bytes 393232 | tf_op jit(solution)/shard_map/reduce_scatter | solution.py:776
  288.3 1.0 convert_element_type.154
  289.3 1.3 fusion.17
  290.7 1.8 fusion.16
  292.6 3.2 collective-permute-start.13
  295.7 2.0 collective-permute-start.14
  299.1 7.8 %collective-permute-start.17 = (bf16[320,256]{1,0:T(8,128)(2,1)S(1)}, bf16[320,256]{1,0:T(8,128)(2,1)S(1)}, u32[]{:S(2)}, u32[]{:S(2)}) collective-permute-start(bf16[320,256]{1,0:T(8,128)(2,1)S(1)} %get-tuple-element.88), channel_id=1, source_target_pairs={{20,0},{24,12},{4,16},{8,28},{0,20},{21,1},{25,13},{5,17},{9,29},{... | collective-permute-start | bytes 491528 | tf_op jit(solution)/shard_map/ppermute | solution.py:837
  306.9 1.3 collective-permute-start.18
  308.2 5.8 %collective-permute-start.19 = (bf16[320,256]{1,0:T(8,128)(2,1)S(1)}, bf16[320,256]{1,0:T(8,128)(2,1)S(1)}, u32[]{:S(2)}, u32[]{:S(2)}) collective-permute-start(bf16[320,256]{1,0:T(8,128)(2,1)S(1)} %get-tuple-element.86), channel_id=1, source_target_pairs={{28,0},{16,12},{12,16},{0,28},{8,20},{29,1},{17,13},{13,17},{1,29}... | collective-permute-start | bytes 491528 | tf_op jit(solution)/shard_map/ppermute | solution.py:837
  314.1 6.2 %collective-permute-done.17.refs_5_ = bf16[320,256]{1,0:T(8,128)(2,1)S(1)} collective-permute-done((bf16[320,256]{1,0:T(8,128)(2,1)S(1)}, bf16[320,256]{1,0:T(8,128)(2,1)S(1)}, u32[]{:S(2)}, u32[]{:S(2)}) %collective-permute-start.17) | collective-permute-done | bytes 163872 | tf_op jit(solution)/shard_map/ppermute | solution.py:837
  320.3 3.5 collective-permute-done.18.refs_6_
  323.8 3.5 collective-permute-done.19.refs_7_
  327.3 1.4 collect.1
  330.0 1.2 constant_dynamic-slice_fusion.2.refs_2_.refs_8_
  331.9 1.3 collective-permute-start.7
  336.1 1.5 collective-permute-done.8
  337.7 2.4 collective-permute-done.9
  340.1 1.7 collective-permute-start.10
  341.7 1.3 dynamic-slice_bitcast_fusion.6
  345.3 1.5 slice-done
  346.7 1.4 copy.43
  348.2 2.3 broadcast_multiply_fusion
  350.5 20.2 %all-gather.10.cloned.1.call-done.g_ref = bf16[1024,2560]{1,0:T(8,128)(2,1)} async-done(((bf16[256,2560]{1,0:T(8,128)(2,1)}), bf16[1024,2560]{1,0:T(8,128)(2,1)}) %all-gather.10.cloned.1.call-update) | async-done | bytes 5242896 | tf_op jit(solution)/shard_map/all_gather | solution.py:684
  370.6 2.5 copy-done
  373.1 47.7 %orthogonal.1.g_ref = bf16[256,2560]{1,0:T(8,128)(2,1)S(1)} custom-call(s32[2]{0:T(128)S(1)} %pad_add_fusion.own_ref, bf16[1024,2560]{1,0:T(8,128)(2,1)S(1)} %copy-done, f32[16,56,384]{2,1,0:T(8,128)S(1)} %bitcast.195, f32[1,1]{1,0:T(1,128)} %div.31.refs_1_, f32[3,256,256]{2,1,0:T(8,128)S(1)} %constant_dynamic-slice_fusion.2.refs_2_.refs_8_, ...), custom_call_target="tpu_custom_call" | custom-call | flops 49999998976 | bytes 6291456 | tf_op jit(solution)/shard_map/orthogonal/pallas_call | solution.py:580
  421.3 1.3 collective-permute-start.20
  422.6 1.3 collective-permute-start.21
  425.3 1.3 collective-permute-start.24
  426.6 2.2 collective-permute-done.20.refs_1_
  428.8 1.3 collective-permute-start.25
  430.1 1.3 collective-permute-start.26
  432.3 18.0 %collective-permute-done.24.refs_5_ = bf16[320,256]{1,0:T(8,128)(2,1)S(1)} collective-permute-done((bf16[320,256]{1,0:T(8,128)(2,1)S(1)}, bf16[320,256]{1,0:T(8,128)(2,1)S(1)}, u32[]{:S(2)}, u32[]{:S(2)}) %collective-permute-start.24) | collective-permute-done | bytes 163872 | tf_op jit(solution)/shard_map/ppermute | solution.py:862
  450.6 17.5 %collective-permute-done.26.refs_7_ = bf16[320,256]{1,0:T(8,128)(2,1)S(1)} collective-permute-done((bf16[320,256]{1,0:T(8,128)(2,1)S(1)}, bf16[320,256]{1,0:T(8,128)(2,1)S(1)}, u32[]{:S(2)}, u32[]{:S(2)}) %collective-permute-start.26) | collective-permute-done | bytes 163872 | tf_op jit(solution)/shard_map/ppermute | solution.py:862
  468.0 1.3 finish.1
  (107 shorter events, 26.4 us)
Async XLA Ops:
  7.2 5.5 %copy-start.6 = (s32[16,56,32]{1,2,0:T(8,128)S(1)}, s32[16,56,32]{1,2,0:T(8,128)}, u32[]{:S(2)}) copy-start(s32[16,56,32]{1,2,0:T(8,128)} %param.11) | copy-start | bytes 344068
  10.5 35.6 %collective-permute-start.1 = (bf16[3,1024,256]{2,1,0:T(8,128)(2,1)}, bf16[3,1024,256]{2,1,0:T(8,128)(2,1)}, u32[]{:S(2)}, u32[]{:S(2)}) collective-permute-start(bf16[3,1024,256]{2,1,0:T(8,128)(2,1)} %slice.186.refs_0_), channel_id=1, source_target_pairs={{0,2},{1,3},{2,0},{3,1},{4,6},{5,7},{6,4},{7,5},{8,10},{9,11},{10,... | collective-permute-start | bytes 4718600 | tf_op jit(solution)/shard_map/ppermute | solution.py:693
  11.7 60.3 %collective-permute-start = (bf16[3,1024,256]{2,1,0:T(8,128)(2,1)}, bf16[3,1024,256]{2,1,0:T(8,128)(2,1)}, u32[]{:S(2)}, u32[]{:S(2)}) collective-permute-start(bf16[3,1024,256]{2,1,0:T(8,128)(2,1)} %slice.186.refs_0_), channel_id=1, source_target_pairs={{0,1},{1,0},{2,3},{3,2},{4,5},{5,4},{6,7},{7,6},{8,9},{9,8},{10,11... | collective-permute-start | bytes 4718600 | tf_op jit(solution)/shard_map/ppermute | solution.py:693
  22.2 4.5 copy-start.8
  22.2 49.8 %all-to-all-start = ((bf16[4,28,8,768]{3,2,1,0:T(8,128)(2,1)}), bf16[4,28,8,768]{3,2,1,0:T(8,128)(2,1)}, u32[]{:S(2)}, u32[]{:S(2)}) async-start(bf16[4,28,8,768]{3,2,1,0:T(8,128)(2,1)} %bitcast.7), calls=%async_computation | async-start | bytes 2752512 | tf_op jit(solution)/shard_map/all_to_all | solution.py:687
  26.6 105.6 %all-gather.8.cloned.1.call-start = ((), (), s32[]{:S(2)}) async-start(), calls=%async_computation.7 | async-start | bytes 9175040 | tf_op jit(solution)/shard_map/all_gather | solution.py:684
  28.0 34.6 %collective-permute-start.3 = (f32[8,128]{1,0:T(8,128)S(1)}, f32[8,128]{1,0:T(8,128)S(1)}, u32[]{:S(2)}, u32[]{:S(2)}) collective-permute-start(f32[8,128]{1,0:T(8,128)S(1)} %broadcast_in_dim.7), channel_id=1, source_target_pairs={{0,4},{4,0},{1,5},{5,1},{2,6},{6,2},{3,7},{7,3},{8,12},{12,8},{9,1... | collective-permute-start | bytes 12296 | tf_op jit(solution)/shard_map/ppermute | solution.py:738
  33.6 18.3 %copy-start.2 = (f32[2560,256]{1,0:T(8,128)S(1)}, f32[2560,256]{1,0:T(8,128)}, u32[]{:S(2)}) copy-start(f32[2560,256]{1,0:T(8,128)} %param.14) | copy-start | bytes 7864324
  46.1 25.9 %collective-permute-start.2 = (bf16[3,1024,256]{2,1,0:T(8,128)(2,1)}, bf16[3,1024,256]{2,1,0:T(8,128)(2,1)}, u32[]{:S(2)}, u32[]{:S(2)}) collective-permute-start(bf16[3,1024,256]{2,1,0:T(8,128)(2,1)} %collective-permute-done.1.refs_2_), channel_id=1, source_target_pairs={{0,1},{1,0},{2,3},{3,2},{4,5},{5,4},{6,7},{7,6},{8,9},{9,8},{10,11... | collective-permute-start | bytes 4718600 | tf_op jit(solution)/shard_map/ppermute | solution.py:693
  52.0 2.3 copy-start.3
  63.3 2.5 collective-permute-start.4
  66.5 4.3 collective-permute-start.5
  72.8 124.9 %all-gather.6.cloned.1.call-start = ((), (), s32[]{:S(2)}) async-start(), calls=%async_computation.4 | async-start | bytes 9175040 | tf_op jit(solution)/shard_map/all_gather | solution.py:684
  131.0 10.9 %collective-permute-start.11 = (bf16[224,1024]{1,0:T(8,128)(2,1)}, bf16[224,1024]{1,0:T(8,128)(2,1)S(1)}, u32[]{:S(2)}, u32[]{:S(2)}) collective-permute-start(bf16[224,1024]{1,0:T(8,128)(2,1)} %bitcast.214), channel_id=1, source_target_pairs={{0,4},{4,0},{1,5},{5,1},{2,6},{6,2},{3,7},{7,3},{8,12},{12,8},{9,1... | collective-permute-start | bytes 1376264 | tf_op jit(solution)/shard_map/ppermute | solution.py:749
  142.7 113.1 %reduce-scatter.3.cloned.1.call-start = ((), (), s32[]{:S(2)}) async-start(), calls=%async_computation.5 | async-start | bytes 2293760 | tf_op jit(solution)/shard_map/reduce_scatter | solution.py:776
  203.8 1.0 slice-start.1
  203.8 1.5 slice-start.2
  205.3 2.4 copy-start.4
  206.7 81.6 %reduce-scatter.5.cloned.1.call-start = ((), (), s32[]{:S(2)}) async-start(), calls=%async_computation.6 | async-start | bytes 1966080 | tf_op jit(solution)/shard_map/reduce_scatter | solution.py:776
  255.7 1.5 copy-start.7
  255.7 17.3 %copy-start.5 = (bf16[1,2,448,256]{3,2,1,0:T(8,128)(2,1)S(1)}, bf16[1,2,448,256]{3,2,1,0:T(8,128)(2,1)}, u32[]{:S(2)}) copy-start(bf16[1,2,448,256]{3,2,1,0:T(8,128)(2,1)} %reduce-scatter.3.cloned.1.call-done) | copy-start | bytes 1376260
  255.8 114.9 %all-gather.10.cloned.1.call-start = ((), (), s32[]{:S(2)}) async-start(), calls=%async_computation.8 | async-start | bytes 6553600 | tf_op jit(solution)/shard_map/all_gather | solution.py:684
  256.8 16.2 %collective-permute-start.12 = (bf16[448,256]{1,0:T(8,128)(2,1)S(1)}, bf16[448,256]{1,0:T(8,128)(2,1)S(1)}, u32[]{:S(2)}, u32[]{:S(2)}) collective-permute-start(bf16[448,256]{1,0:T(8,128)(2,1)S(1)} %dynamic-slice_bitcast_fusion.2), channel_id=1, source_target_pairs={{0,4},{4,0},{1,5},{5,1},{2,6},{6,2},{3,7},{7,3},{8,12},{12,8},{9,1... | collective-permute-start | bytes 688136 | tf_op jit(solution)/shard_map/ppermute | solution.py:787
  292.6 14.4 %collective-permute-start.13 = (bf16[320,256]{1,0:T(8,128)(2,1)S(1)}, bf16[320,256]{1,0:T(8,128)(2,1)S(1)}, u32[]{:S(2)}, u32[]{:S(2)}) collective-permute-start(bf16[320,256]{1,0:T(8,128)(2,1)S(1)} %get-tuple-element.92), channel_id=1, source_target_pairs={{4,0},{8,12},{20,16},{24,28},{16,20},{5,1},{9,13},{21,17},{25,29},... | collective-permute-start | bytes 491528 | tf_op jit(solution)/shard_map/ppermute | solution.py:837
  295.7 12.5 %collective-permute-start.14 = (bf16[320,256]{1,0:T(8,128)(2,1)S(1)}, bf16[320,256]{1,0:T(8,128)(2,1)S(1)}, u32[]{:S(2)}, u32[]{:S(2)}) collective-permute-start(bf16[320,256]{1,0:T(8,128)(2,1)S(1)} %get-tuple-element.91), channel_id=1, source_target_pairs={{8,0},{4,12},{24,16},{20,28},{28,20},{9,1},{5,13},{25,17},{21,29},... | collective-permute-start | bytes 491528 | tf_op jit(solution)/shard_map/ppermute | solution.py:837
  297.7 16.3 %collective-permute-start.15 = (bf16[320,256]{1,0:T(8,128)(2,1)S(1)}, bf16[320,256]{1,0:T(8,128)(2,1)S(1)}, u32[]{:S(2)}, u32[]{:S(2)}) collective-permute-start(bf16[320,256]{1,0:T(8,128)(2,1)S(1)} %get-tuple-element.90), channel_id=1, source_target_pairs={{12,0},{0,12},{28,16},{16,28},{24,20},{13,1},{1,13},{29,17},{17,29... | collective-permute-start | bytes 491528 | tf_op jit(solution)/shard_map/ppermute | solution.py:837
  298.4 15.6 %collective-permute-start.16 = (bf16[320,256]{1,0:T(8,128)(2,1)S(1)}, bf16[320,256]{1,0:T(8,128)(2,1)S(1)}, u32[]{:S(2)}, u32[]{:S(2)}) collective-permute-start(bf16[320,256]{1,0:T(8,128)(2,1)S(1)} %get-tuple-element.89), channel_id=1, source_target_pairs={{16,0},{28,12},{0,16},{12,28},{4,20},{17,1},{29,13},{1,17},{13,29}... | collective-permute-start | bytes 491528 | tf_op jit(solution)/shard_map/ppermute | solution.py:837
  299.1 21.2 %collective-permute-start.17 = (bf16[320,256]{1,0:T(8,128)(2,1)S(1)}, bf16[320,256]{1,0:T(8,128)(2,1)S(1)}, u32[]{:S(2)}, u32[]{:S(2)}) collective-permute-start(bf16[320,256]{1,0:T(8,128)(2,1)S(1)} %get-tuple-element.88), channel_id=1, source_target_pairs={{20,0},{24,12},{4,16},{8,28},{0,20},{21,1},{25,13},{5,17},{9,29},{... | collective-permute-start | bytes 491528 | tf_op jit(solution)/shard_map/ppermute | solution.py:837
  306.9 16.8 %collective-permute-start.18 = (bf16[320,256]{1,0:T(8,128)(2,1)S(1)}, bf16[320,256]{1,0:T(8,128)(2,1)S(1)}, u32[]{:S(2)}, u32[]{:S(2)}) collective-permute-start(bf16[320,256]{1,0:T(8,128)(2,1)S(1)} %get-tuple-element.87), channel_id=1, source_target_pairs={{24,0},{20,12},{8,16},{4,28},{12,20},{25,1},{21,13},{9,17},{5,29},... | collective-permute-start | bytes 491528 | tf_op jit(solution)/shard_map/ppermute | solution.py:837
  308.2 19.0 %collective-permute-start.19 = (bf16[320,256]{1,0:T(8,128)(2,1)S(1)}, bf16[320,256]{1,0:T(8,128)(2,1)S(1)}, u32[]{:S(2)}, u32[]{:S(2)}) collective-permute-start(bf16[320,256]{1,0:T(8,128)(2,1)S(1)} %get-tuple-element.86), channel_id=1, source_target_pairs={{28,0},{16,12},{12,16},{0,28},{8,20},{29,1},{17,13},{13,17},{1,29}... | collective-permute-start | bytes 491528 | tf_op jit(solution)/shard_map/ppermute | solution.py:837
  329.4 1.8 collective-permute-start.6
  331.9 2.5 collective-permute-start.7
  335.1 2.5 collective-permute-start.8
  337.6 2.5 collective-permute-start.9
  340.1 3.4 collective-permute-start.10
  345.2 1.5 slice-start
  350.5 70.4 %copy-start.1 = (f32[4,4,56,384]{3,2,1,0:T(8,128)}, f32[4,4,56,384]{3,2,1,0:T(8,128)S(1)}, u32[]{:S(2)}) copy-start(f32[4,4,56,384]{3,2,1,0:T(8,128)S(1)} %broadcast_multiply_fusion) | copy-start | bytes 4128772
  370.6 2.5 copy-start
  421.3 7.4 %collective-permute-start.20 = (bf16[320,256]{1,0:T(8,128)(2,1)S(1)}, bf16[320,256]{1,0:T(8,128)(2,1)S(1)}, u32[]{:S(2)}, u32[]{:S(2)}) collective-permute-start(bf16[320,256]{1,0:T(8,128)(2,1)S(1)} %get-tuple-element.84), channel_id=1, source_target_pairs={{0,4},{12,8},{16,20},{28,24},{20,16},{1,5},{13,9},{17,21},{29,25},... | collective-permute-start | bytes 491528 | tf_op jit(solution)/shard_map/ppermute | solution.py:862
  422.6 7.4 %collective-permute-start.21 = (bf16[320,256]{1,0:T(8,128)(2,1)S(1)}, bf16[320,256]{1,0:T(8,128)(2,1)S(1)}, u32[]{:S(2)}, u32[]{:S(2)}) collective-permute-start(bf16[320,256]{1,0:T(8,128)(2,1)S(1)} %get-tuple-element.83), channel_id=1, source_target_pairs={{0,8},{12,4},{16,24},{28,20},{20,28},{1,9},{13,5},{17,25},{29,21},... | collective-permute-start | bytes 491528 | tf_op jit(solution)/shard_map/ppermute | solution.py:862
  423.9 8.4 %collective-permute-start.22 = (bf16[320,256]{1,0:T(8,128)(2,1)S(1)}, bf16[320,256]{1,0:T(8,128)(2,1)S(1)}, u32[]{:S(2)}, u32[]{:S(2)}) collective-permute-start(bf16[320,256]{1,0:T(8,128)(2,1)S(1)} %get-tuple-element.82), channel_id=1, source_target_pairs={{0,12},{12,0},{16,28},{28,16},{20,24},{1,13},{13,1},{17,29},{29,17... | collective-permute-start | bytes 491528 | tf_op jit(solution)/shard_map/ppermute | solution.py:862
  424.6 7.7 %collective-permute-start.23 = (bf16[320,256]{1,0:T(8,128)(2,1)S(1)}, bf16[320,256]{1,0:T(8,128)(2,1)S(1)}, u32[]{:S(2)}, u32[]{:S(2)}) collective-permute-start(bf16[320,256]{1,0:T(8,128)(2,1)S(1)} %get-tuple-element.81), channel_id=1, source_target_pairs={{0,16},{12,28},{16,0},{28,12},{20,4},{1,17},{13,29},{17,1},{29,13}... | collective-permute-start | bytes 491528 | tf_op jit(solution)/shard_map/ppermute | solution.py:862
  425.3 25.0 %collective-permute-start.24 = (bf16[320,256]{1,0:T(8,128)(2,1)S(1)}, bf16[320,256]{1,0:T(8,128)(2,1)S(1)}, u32[]{:S(2)}, u32[]{:S(2)}) collective-permute-start(bf16[320,256]{1,0:T(8,128)(2,1)S(1)} %get-tuple-element.80), channel_id=1, source_target_pairs={{0,20},{12,24},{16,4},{28,8},{20,0},{1,21},{13,25},{17,5},{29,9},{... | collective-permute-start | bytes 491528 | tf_op jit(solution)/shard_map/ppermute | solution.py:862
  428.8 21.8 %collective-permute-start.25 = (bf16[320,256]{1,0:T(8,128)(2,1)S(1)}, bf16[320,256]{1,0:T(8,128)(2,1)S(1)}, u32[]{:S(2)}, u32[]{:S(2)}) collective-permute-start(bf16[320,256]{1,0:T(8,128)(2,1)S(1)} %get-tuple-element.79), channel_id=1, source_target_pairs={{0,24},{12,20},{16,8},{28,4},{20,12},{1,25},{13,21},{17,9},{29,5},... | collective-permute-start | bytes 491528 | tf_op jit(solution)/shard_map/ppermute | solution.py:862
  430.1 37.9 %collective-permute-start.26 = (bf16[320,256]{1,0:T(8,128)(2,1)S(1)}, bf16[320,256]{1,0:T(8,128)(2,1)S(1)}, u32[]{:S(2)}, u32[]{:S(2)}) collective-permute-start(bf16[320,256]{1,0:T(8,128)(2,1)S(1)} %get-tuple-element.78), channel_id=1, source_target_pairs={{0,28},{12,16},{16,12},{28,0},{20,8},{1,29},{13,17},{17,13},{29,1}... | collective-permute-start | bytes 491528 | tf_op jit(solution)/shard_map/ppermute | solution.py:862
Sparse Core Ops, SparseCore 0:
  72.9 54.6 all-gather.7
  142.8 54.7 all-gather.5
  206.8 39.4 reduce-scatter.2
  255.9 32.3 reduce-scatter.4
  328.9 41.7 all-gather.9
where the time goes:
time: 485 us; the launch traced here: 477 us
  Pallas kernels  186 us (38%)
  waiting for transfers between devices  105 us (22%)
  starting transfers between devices  48 us (10%)
  blocking collectives  43.4 us (9%)
  between operations  33 us (7%)
  local copies, waits for them, and re-layouts  32.8 us (7%)
  other arithmetic  20.3 us (4%)
  matrix products  8.65 us (2%)
    pallas_call x1, Pallas kernels, run_forward(): pl.pallas_call(functools.partial(scan_forward, seqs, CHUNK), out_shape=[j...  57.2 us
    pallas_call x1, Pallas kernels, run_backward(): pl.pallas_call(functools.partial(scan_backward, seqs, CHUNK), out_shape=j...  54.4 us
    pallas_call x1, Pallas kernels, run_orthogonal(): pl.pallas_call(functools.partial(orthogonal_block, base, 512), out_shape=...  47.7 us
    all_to_all x1, blocking collectives, exchange(): return lax.all_to_all(block, axis, 0, 0, tiled=True)  39.3 us
    ppermute x7, waiting for transfers between devices, on_device(): pieces.append(lax.ppermute(dealt[step], ('dz', 'dx'), pairs))  37.9 us
    ppermute x7, starting transfers between devices, on_device(): block = lax.ppermute(block, ('dz', 'dx'), [(d ^ step, d) for d in owners])  21.4 us
    all_gather x3, waiting for transfers between devices, gather(): return lax.all_gather(block, 'tp', axis=0, tiled=False)  20.2 us
    reduce_scatter x2, waiting for transfers between devices, share_rows(): return lax.psum_scatter(block, 'dz', scatter_dimension=0, tiled=True)[0]  13.6 us
  transfers between devices with their start and end apart: 33, of which 16 were waited for; matrix products, arithmetic and copies ran while one was open for 9% of the time, Pallas kernels for 27%

commit v1 on v0

--- a/solution.py
+++ b/solution.py
@@ -3,6 +3,7 @@
 
 import jax
 import jax.numpy as jnp
+import numpy as np
 from jax import lax
 from jax.experimental import pallas as pl
 from jax.experimental.pallas import tpu as pltpu
@@ -198,11 +199,17 @@
             store.wait()
 
 
-def head_block(h_ref, e_ref, t_ref, m_ref, r_ref, w_hbm, back_ref, d_ref, loss_ref, w_ref, w_sem):
+def head_block(
+    spot_ref, h_ref, p_ref, t_ref, m_ref, r_ref, e_hbm, w_hbm, back_ref, d_ref, loss_ref, w_ref, n_ref, e_ref, w_sem, e_sem
+):
     parts = w_ref.shape[0]
+    embed = copy(e_hbm.at[spot_ref[0]], n_ref, e_sem)
+    embed.start()
     loads = [copy(w_hbm.at[p], w_ref.at[p], w_sem.at[p]) for p in range(parts)]
     for load in loads:
         load.start()
+    embed.wait()
+    e_ref[...] = dot(p_ref[...], n_ref[...]).astype(bf16)
     units = w_ref.shape[2]
     rows = h_ref.shape[0]
     low = h_ref[...]
@@ -238,7 +245,7 @@
     d_ref[...] = direct
 
 
-def head_grads(spot_ref, scale_ref, r_hbm, e_hbm, earlier_ref, o_ref, h_ref, r_ref, e_ref, sems):
+def head_grads(spot_ref, scale_ref, p_ref, r_hbm, e_hbm, earlier_ref, o_ref, h_ref, r_ref, e_ref, sems):
     parts, rows = e_ref.shape[0], e_ref.shape[1]
     units = o_ref.shape[1]
     frames = parts * rows
@@ -260,6 +267,9 @@
         grad = (dot_tn(h_ref[:, :, spot].reshape(frames, 256), both) * scale).astype(bf16)
         o_ref[m * 256 : (m + 1) * 256] = grad[:, :units]
         o_ref[H + E + m * 256 : H + E + (m + 1) * 256] = grad[:, units:]
+    post = jnp.concatenate(
+        [dot_tn(p_ref[...], r_ref[p, 1]).astype(bf16) for p in range(parts)], axis=0
+    )
     loads[2].wait()
     for m in range(E // 256):
         spot = slice(m * 256, (m + 1) * 256)
@@ -490,7 +500,7 @@
     )(direct, factors, rest, turned)
 
 
-def run_heads(hidden, embed, target, mask, mask_row, weights):
+def run_heads(spot, hidden, order, target, mask, mask_row, embed, weights):
     rows = hidden.shape[0]
     return pl.pallas_call(
         head_block,
@@ -499,16 +509,19 @@
             jax.ShapeDtypeStruct((rows, H), f32),
             jax.ShapeDtypeStruct((1, 1), f32),
         ],
-        in_specs=in_vmem(5) + anywhere(1),
+        in_specs=in_smem(1) + in_vmem(5) + anywhere(2),
         out_specs=in_vmem(3),
         scratch_shapes=[
             pltpu.VMEM(weights.shape, bf16),
+            pltpu.VMEM((rows, E), bf16),
+            pltpu.VMEM((rows, E), bf16),
             pltpu.SemaphoreType.DMA((weights.shape[0],)),
+            pltpu.SemaphoreType.DMA,
         ],
         compiler_params=pltpu.CompilerParams(vmem_limit_bytes=LARGE),
         cost_estimate=cost(1e10, 12 * mib),
         name="heads",
-    )(hidden, embed, target, mask, mask_row, weights)
+    )(spot, hidden, order, target, mask, mask_row, embed, weights)
 
 
 def in_smem(count):
@@ -519,13 +532,13 @@
     return [pl.BlockSpec(memory_space=pl.ANY)] * count
 
 
-def run_head_grads(spot, scale, everyone, embed, earlier):
+def run_head_grads(spot, scale, order, everyone, embed, earlier):
     parts, rows = embed.shape[:2]
     units = H // parts
     return pl.pallas_call(
         head_grads,
         out_shape=jax.ShapeDtypeStruct((H + E + H, units), bf16),
-        in_specs=in_smem(2) + anywhere(3),
+        in_specs=in_smem(2) + in_vmem(1) + anywhere(3),
         out_specs=in_vmem(1)[0],
         scratch_shapes=[
             pltpu.VMEM((parts, rows, H), bf16),
@@ -536,7 +549,7 @@
         compiler_params=pltpu.CompilerParams(vmem_limit_bytes=LARGE),
         cost_estimate=cost(4e9, 12 * mib),
         name="head_grads",
-    )(spot, scale, everyone, embed, earlier)
+    )(spot, scale, order, everyone, embed, earlier)
 
 
 def run_gru_grads(spot, scale, onehot, everyone, back, earlier, dz_count):
@@ -712,16 +725,21 @@
         [dot(onehot, gru_input[k, :Z].astype(bf16)).astype(bf16) for k in range(3)], axis=1
     ).reshape(tp_count, packs, PACK, 3 * units)
     input_part = exchange(input_part, "tp")
-    embed_rows = jnp.swapaxes(embeddings.reshape(tp_count, seqs, FRAMES, E), 1, 2)
-    embed_rows = embed_rows.reshape(tp_count, rows, E)
-    pair_samples = lax.all_gather(by_part, "dx", axis=0, tiled=False)
+    embed_rows = embeddings.reshape(tp_count, rows, E)
+    order = np.zeros((rows, rows), np.float32)
+    order[np.arange(rows), np.arange(rows) % seqs * FRAMES + np.arange(rows) // seqs] = 1.0
+    order = jnp.asarray(order, bf16)
+    swap = [(i, i ^ 1) for i in range(dx_count)]
+    other = lax.ppermute(by_part, "dx", swap)
+    pair_samples = jnp.where(
+        dx_index == 0, jnp.stack([by_part, other]), jnp.stack([other, by_part])
+    )
     half = Z // dx_count
     pair_half = mine(
         pair_samples.reshape(dx_count * tp_count * rows, dz_count // 2, dx_count, -1), 2
     )
     pair_onehot = one_hot(pair_half.reshape(dx_count * tp_count * rows, groups // dx_count))
     pair_onehot = pair_onehot.reshape(dx_count, tp_count * rows, half)
-    own_embed = lax.dynamic_index_in_dim(embed_rows, tp_index, 0, keepdims=False)
     onehot = onehot.reshape(tp_count, rows, Z)
     own_target = lax.dynamic_index_in_dim(onehot, tp_index, 0, keepdims=False)
     positions = jnp.arange(FRAMES, dtype=jnp.int32)
@@ -739,16 +757,22 @@
     frame_count = frame_count[0, 0]
     scale = (1.0 / frame_count).reshape(1)
 
-    early = (head_low, own_embed, own_target, mask_lanes, embed_rows, pair_onehot, scale)
+    early = (head_low, own_target, mask_lanes, pair_onehot, scale)
     weights, input_part, early = lax.optimization_barrier((weights, input_part, early))
-    head_low, own_embed, own_target, mask_lanes, embed_rows, pair_onehot, scale = early
+    head_low, own_target, mask_lanes, pair_onehot, scale = early
     head_full = gather(head_low)
     hidden, factors, rest, turned = run_forward(tp_index.astype(jnp.int32).reshape(1), input_part, weights, seqs)
     hidden = hidden.reshape(rows, H)
-    swap = [(i, i ^ 1) for i in range(dx_count)]
     neighbour = lax.ppermute(hidden, "dx", swap)
     backs, direct, loss_lanes = run_heads(
-        hidden, own_embed, own_target, mask_lanes, frame_mask.reshape(1, rows), head_full
+        tp_index.astype(jnp.int32).reshape(1),
+        hidden,
+        order,
+        own_target,
+        mask_lanes,
+        frame_mask.reshape(1, rows),
+        embed_rows,
+        head_full,
     )
     everyone = gather(lax.dynamic_update_slice(backs, neighbour[None], (1, 0, 0)))
     back = run_backward(
@@ -761,8 +785,7 @@
     all_post = everyone[:, 3]
     spot = jnp.stack([tp_index, dx_index]).astype(jnp.int32)
 
-    head_grad = run_head_grads(spot, scale, everyone, embed_rows, back)
-    own_back, _ = lax.optimization_barrier((own_back, head_grad))
+    head_grad = run_head_grads(spot, scale, order, everyone, embed_rows, back)
 
     head_grad = jnp.concatenate(
         [

time: 485 us -> 474 us (0.977)
  local copies, waits for them, and re-layouts: 32.8 us -> 27.6 us
  transfers between devices with their start and end apart: 33 -> 34, of which waited for: 16 -> 15; matrix products, arithmetic and copies ran while one was open for 9% -> 9% of each run, Pallas kernels for 27% -> 28%
where the time goes in v1:
time: 474 us; the launch traced here: 467 us
  Pallas kernels  188 us (40%)
  waiting for transfers between devices  103 us (22%)
  starting transfers between devices  48.6 us (10%)
  blocking collectives  38.9 us (8%)
  between operations  33.2 us (7%)
  local copies, waits for them, and re-layouts  27.6 us (6%)
  other arithmetic  18.6 us (4%)
  matrix products  9.53 us (2%)
    pallas_call x1, Pallas kernels, run_forward(): pl.pallas_call(functools.partial(scan_forward, seqs, CHUNK), out_shape=[j...  57.2 us
    pallas_call x1, Pallas kernels, run_backward(): pl.pallas_call(functools.partial(scan_backward, seqs, CHUNK), out_shape=j...  54.4 us
    pallas_call x1, Pallas kernels, run_orthogonal(): pl.pallas_call(functools.partial(orthogonal_block, base, 512), out_shape=...  47.7 us
    all_to_all x1, blocking collectives, exchange(): return lax.all_to_all(block, axis, 0, 0, tiled=True)  38.9 us
    ppermute x7, waiting for transfers between devices, on_device(): pieces.append(lax.ppermute(dealt[step], ('dz', 'dx'), pairs))  37.9 us
    ppermute x7, starting transfers between devices, on_device(): block = lax.ppermute(block, ('dz', 'dx'), [(d ^ step, d) for d in owners])  21.4 us
    all_gather x3, waiting for transfers between devices, gather(): return lax.all_gather(block, 'tp', axis=0, tiled=False)  20.1 us
    reduce_scatter x2, waiting for transfers between devices, share_rows(): return lax.psum_scatter(block, 'dz', scatter_dimension=0, tiled=True)[0]  14.2 us
  transfers between devices with their start and end apart: 34, of which 15 were waited for; matrix products, arithmetic and copies ran while one was open for 9% of the time, Pallas kernels for 28%

profile of v1, /device:TPU:9, one launch (start us, length us, event | category | flops | bytes accessed | tf_op | source)
XLA Modules:
  0.0 467.5 jit_solution(6201714095543622610)
XLA Ops:
  7.2 2.1 slice.186.refs_0_
  9.3 1.3 collective-permute-start.1
  10.6 1.0 collective-permute-start
  12.4 1.2 collective-permute-start.3
  13.6 3.1 convert.16
  16.7 3.0 fusion.46
  22.2 1.5 copy.42
  23.8 4.7 %all-to-all-start = ((bf16[4,28,8,768]{3,2,1,0:T(8,128)(2,1)}), bf16[4,28,8,768]{3,2,1,0:T(8,128)(2,1)}, u32[]{:S(2)}, u32[]{:S(2)}) async-start(bf16[4,28,8,768]{3,2,1,0:T(8,128)(2,1)} %bitcast.7), calls=%async_computation | async-start | bytes 2752512 | tf_op jit(solution)/shard_map/all_to_all | solution.py:700
  30.2 1.9 convert_element_type.144
  32.1 12.6 %collective-permute-done.1.refs_2_ = bf16[3,1024,256]{2,1,0:T(8,128)(2,1)} collective-permute-done((bf16[3,1024,256]{2,1,0:T(8,128)(2,1)S(1)}, bf16[3,1024,256]{2,1,0:T(8,128)(2,1)}, u32[]{:S(2)}, u32[]{:S(2)}) %collective-permute-start.1) | collective-permute-done | bytes 1572896 | tf_op jit(solution)/shard_map/ppermute | solution.py:706
  44.7 2.7 collective-permute-start.2
  47.4 1.4 pad_maximum_fusion
  49.6 1.8 dynamic-slice_bitcast_fusion.t_ref
  52.7 2.4 collective-permute-start.6
  55.2 1.1 copy.43
  57.6 1.1 copy.44
  58.9 1.9 compare_convert_fusion
  62.6 57.2 %scan_forward.1 = (bf16[28,8,1024]{2,1,0:T(8,128)(2,1)}, f32[3,28,8,1024]{3,2,1,0:T(8,128)}, f32[28,8,1024]{2,1,0:T(8,128)}, bf16[3072,1024]{1,0:T(8,128)(2,1)}) custom-call(s32[1]{0:T(128)} %bitcast.spot_ref, bf16[4,28,8,768]{3,2,1,0:T(8,128)(2,1)} %all-to-all-done.x_ref, bf16[3,1024,256]{2,1,0:T(8,128)(2,1)} %copy-done.3, ...), custom_call_target="tpu_custom_call" | custom-call | flops 60000002048 | bytes 20971520 | tf_op jit(solution)/shard_map/scan_forward/pallas_call | solution.py:449
  119.8 1.3 collective-permute-start.12
  121.0 10.3 %heads.1 = (bf16[4,224,1024]{2,1,0:T(8,128)(2,1)}, f32[224,1024]{1,0:T(8,128)}, f32[1,1]{1,0:T(1,128)}) custom-call(s32[1]{0:T(128)} %bitcast.spot_ref, bf16[224,1024]{1,0:T(8,128)(2,1)} %bitcast.209, bf16[224,224]{1,0:T(8,128)(2,1)} %constant.146.clone.p_ref, bf16[224,1024]{1,0:T(8,128)(2,1)} %dynamic-slice_bitcast_fusion.t_ref, ...), custom_call_target="tpu_custom_call" | custom-call | flops 10000000000 | bytes 12582912 | tf_op jit(solution)/shard_map/heads/pallas_call | solution.py:505
  132.9 54.4 %scan_backward.1.earlier_ref = bf16[2,4,28,8,768]{4,3,2,1,0:T(8,128)(2,1)} custom-call(f32[28,8,1024]{2,1,0:T(8,128)} %bitcast.210, f32[3,28,8,1024]{3,2,1,0:T(8,128)} %get-tuple-element.47.k_hbm, f32[28,8,1024]{2,1,0:T(8,128)} %get-tuple-element.48.u_hbm, bf16[3072,1024]{1,0:T(8,128)(2,1)} %get-tuple-element.49.t_hbm), custom_call_target="tpu_custom_call" | custom-call | flops 60000002048 | bytes 20971520 | tf_op jit(solution)/shard_map/scan_backward/pallas_call | solution.py:480
  187.3 6.4 %head_grads.1 = bf16[3584,256]{1,0:T(8,128)(2,1)} custom-call(s32[2]{0:T(128)} %pad_add_fusion.1.spot_ref, f32[1]{0:T(128)} %bitcast.17.scale_ref, bf16[224,224]{1,0:T(8,128)(2,1)} %constant.146.clone.p_ref, bf16[4,4,224,1024]{3,2,1,0:T(8,128)(2,1)} %all-gather.6.cloned.1.call-done.r_hbm, bf16[4,224,1536]{2,1,0:T(8,128)(2,1)} %bitcast.207, ...), custom_call_target="tpu_custom_call" | custom-call | flops 4000000000 | bytes 12582912 | tf_op jit(solution)/shard_map/head_grads/pallas_call | solution.py:538
  193.7 1.0 slice-done.1
  195.2 1.4 pad_maximum_fusion.1.earlier_ref
  196.6 1.0 copy-done.2
  197.6 38.9 %all_to_all.10 = bf16[8,224,768]{2,1,0:T(8,128)(2,1)} all-to-all(bf16[8,224,768]{2,1,0:T(8,128)(2,1)S(1)} %bitcast.197), channel_id=1, replica_groups=mesh['dz'=4,'dx'=2,'tp'=4] {'dx','tp'}, dimensions={0} | all-to-all | bytes 5505024 | tf_op jit(solution)/shard_map/all_to_all | solution.py:700
  236.5 8.6 %gru_grads.1 = bf16[4,768,256]{2,1,0:T(8,128)(2,1)} custom-call(s32[2]{0:T(128)} %pad_add_fusion.1.spot_ref, f32[1]{0:T(128)} %bitcast.17.scale_ref, bf16[2,896,512]{2,1,0:T(8,128)(2,1)} %bitcast.194, bf16[4,4,224,1024]{3,2,1,0:T(8,128)(2,1)} %all-gather.6.cloned.1.call-done.r_hbm, bf16[2,4,224,768]{3,2,1,0:T(8,128)(2,1)} %bitcast.193, ...), custom_call_target="tpu_custom_call" | custom-call | flops 4000000000 | bytes 12582912 | tf_op jit(solution)/shard_map/gru_grads/pallas_call | solution.py:559
  245.3 1.0 dynamic-slice_bitcast_fusion.1
  262.8 1.6 add_convert_fusion.4
  264.4 14.2 %reduce-scatter.5.cloned.1.call-done = bf16[1,768,256]{2,1,0:T(8,128)(2,1)} async-done(((bf16[4,768,256]{2,1,0:T(8,128)(2,1)}), bf16[1,768,256]{2,1,0:T(8,128)(2,1)}) %reduce-scatter.5.cloned.1.call-update) | async-done | bytes 393232 | tf_op jit(solution)/shard_map/reduce_scatter | solution.py:799
  278.6 1.0 convert_element_type.154
  279.6 1.3 fusion.17
  281.0 1.8 fusion.16
  282.9 3.1 collective-permute-start.14
  285.9 2.1 collective-permute-start.15
  289.4 7.8 %collective-permute-start.18 = (bf16[320,256]{1,0:T(8,128)(2,1)S(1)}, bf16[320,256]{1,0:T(8,128)(2,1)S(1)}, u32[]{:S(2)}, u32[]{:S(2)}) collective-permute-start(bf16[320,256]{1,0:T(8,128)(2,1)S(1)} %get-tuple-element.82), channel_id=1, source_target_pairs={{20,0},{24,12},{4,16},{8,28},{0,20},{21,1},{25,13},{5,17},{9,29},{... | collective-permute-start | bytes 491528 | tf_op jit(solution)/shard_map/ppermute | solution.py:860
  297.2 1.3 collective-permute-start.19
  298.6 5.8 %collective-permute-start.20 = (bf16[320,256]{1,0:T(8,128)(2,1)S(1)}, bf16[320,256]{1,0:T(8,128)(2,1)S(1)}, u32[]{:S(2)}, u32[]{:S(2)}) collective-permute-start(bf16[320,256]{1,0:T(8,128)(2,1)S(1)} %get-tuple-element.80), channel_id=1, source_target_pairs={{28,0},{16,12},{12,16},{0,28},{8,20},{29,1},{17,13},{13,17},{1,29}... | collective-permute-start | bytes 491528 | tf_op jit(solution)/shard_map/ppermute | solution.py:860
  304.4 6.2 %collective-permute-done.18.refs_5_ = bf16[320,256]{1,0:T(8,128)(2,1)S(1)} collective-permute-done((bf16[320,256]{1,0:T(8,128)(2,1)S(1)}, bf16[320,256]{1,0:T(8,128)(2,1)S(1)}, u32[]{:S(2)}, u32[]{:S(2)}) %collective-permute-start.18) | collective-permute-done | bytes 163872 | tf_op jit(solution)/shard_map/ppermute | solution.py:860
  310.6 3.5 collective-permute-done.19.refs_6_
  314.1 3.5 collective-permute-done.20.refs_7_
  317.6 1.5 collect.1
  320.4 1.2 constant_dynamic-slice_fusion.2.refs_2_.refs_8_
  322.2 1.3 collective-permute-start.8
  323.5 1.0 constant_dynamic-slice_fusion.1.refs_3_.refs_9_
  326.4 1.5 collective-permute-done.9
  328.0 2.4 collective-permute-done.10
  330.4 1.7 collective-permute-start.11
  332.1 1.3 dynamic-slice_bitcast_fusion.5
  335.6 1.5 slice-done
  337.1 1.4 copy.48
  338.6 2.3 broadcast_multiply_fusion
  340.9 20.1 %all-gather.10.cloned.1.call-done.g_ref = bf16[1024,2560]{1,0:T(8,128)(2,1)} async-done(((bf16[256,2560]{1,0:T(8,128)(2,1)}), bf16[1024,2560]{1,0:T(8,128)(2,1)}) %all-gather.10.cloned.1.call-update) | async-done | bytes 5242896 | tf_op jit(solution)/shard_map/all_gather | solution.py:697
  360.9 2.5 copy-done
  363.4 47.7 %orthogonal.1.g_ref = bf16[256,2560]{1,0:T(8,128)(2,1)S(1)} custom-call(s32[2]{0:T(128)S(1)} %pad_add_fusion.own_ref, bf16[1024,2560]{1,0:T(8,128)(2,1)S(1)} %copy-done, f32[16,56,384]{2,1,0:T(8,128)S(1)} %bitcast.191, f32[1,1]{1,0:T(1,128)} %div.31.refs_1_, f32[3,256,256]{2,1,0:T(8,128)S(1)} %constant_dynamic-slice_fusion.2.refs_2_.refs_8_, ...), custom_call_target="tpu_custom_call" | custom-call | flops 49999998976 | bytes 6291456 | tf_op jit(solution)/shard_map/orthogonal/pallas_call | solution.py:593
  411.6 1.3 collective-permute-start.21
  412.9 1.3 collective-permute-start.22
  415.6 1.3 collective-permute-start.25
  416.9 2.2 collective-permute-done.21.refs_1_
  419.1 1.3 collective-permute-start.26
  420.4 1.3 collective-permute-start.27
  422.6 17.9 %collective-permute-done.25.refs_5_ = bf16[320,256]{1,0:T(8,128)(2,1)S(1)} collective-permute-done((bf16[320,256]{1,0:T(8,128)(2,1)S(1)}, bf16[320,256]{1,0:T(8,128)(2,1)S(1)}, u32[]{:S(2)}, u32[]{:S(2)}) %collective-permute-start.25) | collective-permute-done | bytes 163872 | tf_op jit(solution)/shard_map/ppermute | solution.py:885
  440.8 17.5 %collective-permute-done.27.refs_7_ = bf16[320,256]{1,0:T(8,128)(2,1)S(1)} collective-permute-done((bf16[320,256]{1,0:T(8,128)(2,1)S(1)}, bf16[320,256]{1,0:T(8,128)(2,1)S(1)}, u32[]{:S(2)}, u32[]{:S(2)}) %collective-permute-start.27) | collective-permute-done | bytes 163872 | tf_op jit(solution)/shard_map/ppermute | solution.py:885
  458.3 1.3 finish.1
  (107 shorter events, 22.4 us)
Async XLA Ops:
  7.2 4.4 copy-start.6
  9.3 7.5 %copy-start.3 = (bf16[3,1024,256]{2,1,0:T(8,128)(2,1)}, bf16[3,1024,256]{2,1,0:T(8,128)(2,1)S(1)}, u32[]{:S(2)}) copy-start(bf16[3,1024,256]{2,1,0:T(8,128)(2,1)S(1)} %slice.186.refs_0_) | copy-start | bytes 4718596
  9.3 35.4 %collective-permute-start.1 = (bf16[3,1024,256]{2,1,0:T(8,128)(2,1)S(1)}, bf16[3,1024,256]{2,1,0:T(8,128)(2,1)}, u32[]{:S(2)}, u32[]{:S(2)}) collective-permute-start(bf16[3,1024,256]{2,1,0:T(8,128)(2,1)S(1)} %slice.186.refs_0_), channel_id=1, source_target_pairs={{0,2},{1,3},{2,0},{3,1},{4,6},{5,7},{6,4},{7,5},{8,10},{9,11},{10,... | collective-permute-start | bytes 4718600 | tf_op jit(solution)/shard_map/ppermute | solution.py:706
  10.6 50.2 %collective-permute-start = (bf16[3,1024,256]{2,1,0:T(8,128)(2,1)S(1)}, bf16[3,1024,256]{2,1,0:T(8,128)(2,1)}, u32[]{:S(2)}, u32[]{:S(2)}) collective-permute-start(bf16[3,1024,256]{2,1,0:T(8,128)(2,1)S(1)} %slice.186.refs_0_), channel_id=1, source_target_pairs={{0,1},{1,0},{2,3},{3,2},{4,5},{5,4},{6,7},{7,6},{8,9},{9,8},{10,11... | collective-permute-start | bytes 4718600 | tf_op jit(solution)/shard_map/ppermute | solution.py:706
  12.4 45.2 %collective-permute-start.3 = (bf16[896,32]{1,0:T(8,128)(2,1)}, bf16[896,32]{1,0:T(8,128)(2,1)}, u32[]{:S(2)}, u32[]{:S(2)}) collective-permute-start(bf16[896,32]{1,0:T(8,128)(2,1)} %bitcast.3), channel_id=1, source_target_pairs={{0,4},{4,0},{1,5},{5,1},{2,6},{6,2},{3,7},{7,3},{8,12},{12,8},{9,1... | collective-permute-start | bytes 172040 | tf_op jit(solution)/shard_map/ppermute | solution.py:733
  23.8 4.7 %copy-start.8 = (s32[16]{0:T(128)S(1)}, s32[16]{0:T(128)}, u32[]{:S(2)}) copy-start(s32[16]{0:T(128)} %param.13) | copy-start | bytes 196
  23.8 6.4 %copy-start.4 = (f32[1024,256]{1,0:T(8,128)S(1)}, f32[1024,256]{1,0:T(8,128)}, u32[]{:S(2)}) copy-start(f32[1024,256]{1,0:T(8,128)} %param.16) | copy-start | bytes 3145732
  23.8 37.0 %all-to-all-start = ((bf16[4,28,8,768]{3,2,1,0:T(8,128)(2,1)}), bf16[4,28,8,768]{3,2,1,0:T(8,128)(2,1)}, u32[]{:S(2)}, u32[]{:S(2)}) async-start(bf16[4,28,8,768]{3,2,1,0:T(8,128)(2,1)} %bitcast.7), calls=%async_computation | async-start | bytes 2752512 | tf_op jit(solution)/shard_map/all_to_all | solution.py:700
  28.5 92.6 %all-gather.8.cloned.1.call-start = ((), (), s32[]{:S(2)}) async-start(), calls=%async_computation.7 | async-start | bytes 9175040 | tf_op jit(solution)/shard_map/all_gather | solution.py:697
  29.8 19.1 %collective-permute-start.4 = (f32[8,128]{1,0:T(8,128)S(1)}, f32[8,128]{1,0:T(8,128)S(1)}, u32[]{:S(2)}, u32[]{:S(2)}) collective-permute-start(f32[8,128]{1,0:T(8,128)S(1)} %broadcast_in_dim.7), channel_id=1, source_target_pairs={{0,4},{4,0},{1,5},{5,1},{2,6},{6,2},{3,7},{7,3},{8,12},{12,8},{9,1... | collective-permute-start | bytes 12296 | tf_op jit(solution)/shard_map/ppermute | solution.py:756
  44.7 16.1 %collective-permute-start.2 = (bf16[3,1024,256]{2,1,0:T(8,128)(2,1)}, bf16[3,1024,256]{2,1,0:T(8,128)(2,1)}, u32[]{:S(2)}, u32[]{:S(2)}) collective-permute-start(bf16[3,1024,256]{2,1,0:T(8,128)(2,1)} %collective-permute-done.1.refs_2_), channel_id=1, source_target_pairs={{0,1},{1,0},{2,3},{3,2},{4,5},{5,4},{6,7},{7,6},{8,9},{9,8},{10,11... | collective-permute-start | bytes 4718600 | tf_op jit(solution)/shard_map/ppermute | solution.py:706
  49.5 2.6 collective-permute-start.5
  52.7 3.5 collective-permute-start.6
  61.6 125.7 %all-gather.6.cloned.1.call-start = ((), (), s32[]{:S(2)}) async-start(), calls=%async_computation.4 | async-start | bytes 9175040 | tf_op jit(solution)/shard_map/all_gather | solution.py:697
  119.8 11.6 %collective-permute-start.12 = (bf16[224,1024]{1,0:T(8,128)(2,1)}, bf16[224,1024]{1,0:T(8,128)(2,1)S(1)}, u32[]{:S(2)}, u32[]{:S(2)}) collective-permute-start(bf16[224,1024]{1,0:T(8,128)(2,1)} %bitcast.208), channel_id=1, source_target_pairs={{0,4},{4,0},{1,5},{5,1},{2,6},{6,2},{3,7},{7,3},{8,12},{12,8},{9,1... | collective-permute-start | bytes 1376264 | tf_op jit(solution)/shard_map/ppermute | solution.py:766
  132.2 113.0 %reduce-scatter.3.cloned.1.call-start = ((), (), s32[]{:S(2)}) async-start(), calls=%async_computation.5 | async-start | bytes 2293760 | tf_op jit(solution)/shard_map/reduce_scatter | solution.py:799
  193.7 1.0 slice-start.1
  193.7 1.5 slice-start.2
  195.1 2.4 copy-start.2
  196.5 82.0 %reduce-scatter.5.cloned.1.call-start = ((), (), s32[]{:S(2)}) async-start(), calls=%async_computation.6 | async-start | bytes 1966080 | tf_op jit(solution)/shard_map/reduce_scatter | solution.py:799
  245.1 1.5 copy-start.7
  245.2 17.6 %copy-start.5 = (bf16[1,2,448,256]{3,2,1,0:T(8,128)(2,1)S(1)}, bf16[1,2,448,256]{3,2,1,0:T(8,128)(2,1)}, u32[]{:S(2)}) copy-start(bf16[1,2,448,256]{3,2,1,0:T(8,128)(2,1)} %reduce-scatter.3.cloned.1.call-done) | copy-start | bytes 1376260
  245.2 115.7 %all-gather.10.cloned.1.call-start = ((), (), s32[]{:S(2)}) async-start(), calls=%async_computation.8 | async-start | bytes 6553600 | tf_op jit(solution)/shard_map/all_gather | solution.py:697
  246.3 16.5 %collective-permute-start.13 = (bf16[448,256]{1,0:T(8,128)(2,1)S(1)}, bf16[448,256]{1,0:T(8,128)(2,1)S(1)}, u32[]{:S(2)}, u32[]{:S(2)}) collective-permute-start(bf16[448,256]{1,0:T(8,128)(2,1)S(1)} %dynamic-slice_bitcast_fusion.1), channel_id=1, source_target_pairs={{0,4},{4,0},{1,5},{5,1},{2,6},{6,2},{3,7},{7,3},{8,12},{12,8},{9,1... | collective-permute-start | bytes 688136 | tf_op jit(solution)/shard_map/ppermute | solution.py:810
  282.9 14.4 %collective-permute-start.14 = (bf16[320,256]{1,0:T(8,128)(2,1)S(1)}, bf16[320,256]{1,0:T(8,128)(2,1)S(1)}, u32[]{:S(2)}, u32[]{:S(2)}) collective-permute-start(bf16[320,256]{1,0:T(8,128)(2,1)S(1)} %get-tuple-element.86), channel_id=1, source_target_pairs={{4,0},{8,12},{20,16},{24,28},{16,20},{5,1},{9,13},{21,17},{25,29},... | collective-permute-start | bytes 491528 | tf_op jit(solution)/shard_map/ppermute | solution.py:860
  285.9 12.6 %collective-permute-start.15 = (bf16[320,256]{1,0:T(8,128)(2,1)S(1)}, bf16[320,256]{1,0:T(8,128)(2,1)S(1)}, u32[]{:S(2)}, u32[]{:S(2)}) collective-permute-start(bf16[320,256]{1,0:T(8,128)(2,1)S(1)} %get-tuple-element.85), channel_id=1, source_target_pairs={{8,0},{4,12},{24,16},{20,28},{28,20},{9,1},{5,13},{25,17},{21,29},... | collective-permute-start | bytes 491528 | tf_op jit(solution)/shard_map/ppermute | solution.py:860
  288.1 16.3 %collective-permute-start.16 = (bf16[320,256]{1,0:T(8,128)(2,1)S(1)}, bf16[320,256]{1,0:T(8,128)(2,1)S(1)}, u32[]{:S(2)}, u32[]{:S(2)}) collective-permute-start(bf16[320,256]{1,0:T(8,128)(2,1)S(1)} %get-tuple-element.84), channel_id=1, source_target_pairs={{12,0},{0,12},{28,16},{16,28},{24,20},{13,1},{1,13},{29,17},{17,29... | collective-permute-start | bytes 491528 | tf_op jit(solution)/shard_map/ppermute | solution.py:860
  288.7 15.6 %collective-permute-start.17 = (bf16[320,256]{1,0:T(8,128)(2,1)S(1)}, bf16[320,256]{1,0:T(8,128)(2,1)S(1)}, u32[]{:S(2)}, u32[]{:S(2)}) collective-permute-start(bf16[320,256]{1,0:T(8,128)(2,1)S(1)} %get-tuple-element.83), channel_id=1, source_target_pairs={{16,0},{28,12},{0,16},{12,28},{4,20},{17,1},{29,13},{1,17},{13,29}... | collective-permute-start | bytes 491528 | tf_op jit(solution)/shard_map/ppermute | solution.py:860
  289.4 21.2 %collective-permute-start.18 = (bf16[320,256]{1,0:T(8,128)(2,1)S(1)}, bf16[320,256]{1,0:T(8,128)(2,1)S(1)}, u32[]{:S(2)}, u32[]{:S(2)}) collective-permute-start(bf16[320,256]{1,0:T(8,128)(2,1)S(1)} %get-tuple-element.82), channel_id=1, source_target_pairs={{20,0},{24,12},{4,16},{8,28},{0,20},{21,1},{25,13},{5,17},{9,29},{... | collective-permute-start | bytes 491528 | tf_op jit(solution)/shard_map/ppermute | solution.py:860
  297.2 16.9 %collective-permute-start.19 = (bf16[320,256]{1,0:T(8,128)(2,1)S(1)}, bf16[320,256]{1,0:T(8,128)(2,1)S(1)}, u32[]{:S(2)}, u32[]{:S(2)}) collective-permute-start(bf16[320,256]{1,0:T(8,128)(2,1)S(1)} %get-tuple-element.81), channel_id=1, source_target_pairs={{24,0},{20,12},{8,16},{4,28},{12,20},{25,1},{21,13},{9,17},{5,29},... | collective-permute-start | bytes 491528 | tf_op jit(solution)/shard_map/ppermute | solution.py:860
  298.6 19.0 %collective-permute-start.20 = (bf16[320,256]{1,0:T(8,128)(2,1)S(1)}, bf16[320,256]{1,0:T(8,128)(2,1)S(1)}, u32[]{:S(2)}, u32[]{:S(2)}) collective-permute-start(bf16[320,256]{1,0:T(8,128)(2,1)S(1)} %get-tuple-element.80), channel_id=1, source_target_pairs={{28,0},{16,12},{12,16},{0,28},{8,20},{29,1},{17,13},{13,17},{1,29}... | collective-permute-start | bytes 491528 | tf_op jit(solution)/shard_map/ppermute | solution.py:860
  319.7 1.8 collective-permute-start.7
  322.2 2.5 collective-permute-start.8
  325.4 2.5 collective-permute-start.9
  327.9 2.5 collective-permute-start.10
  330.4 3.4 collective-permute-start.11
  335.6 1.5 slice-start
  340.9 70.3 %copy-start.1 = (f32[4,4,56,384]{3,2,1,0:T(8,128)}, f32[4,4,56,384]{3,2,1,0:T(8,128)S(1)}, u32[]{:S(2)}) copy-start(f32[4,4,56,384]{3,2,1,0:T(8,128)S(1)} %broadcast_multiply_fusion) | copy-start | bytes 4128772
  360.9 2.5 copy-start
  411.6 7.4 %collective-permute-start.21 = (bf16[320,256]{1,0:T(8,128)(2,1)S(1)}, bf16[320,256]{1,0:T(8,128)(2,1)S(1)}, u32[]{:S(2)}, u32[]{:S(2)}) collective-permute-start(bf16[320,256]{1,0:T(8,128)(2,1)S(1)} %get-tuple-element.78), channel_id=1, source_target_pairs={{0,4},{12,8},{16,20},{28,24},{20,16},{1,5},{13,9},{17,21},{29,25},... | collective-permute-start | bytes 491528 | tf_op jit(solution)/shard_map/ppermute | solution.py:885
  412.9 7.4 %collective-permute-start.22 = (bf16[320,256]{1,0:T(8,128)(2,1)S(1)}, bf16[320,256]{1,0:T(8,128)(2,1)S(1)}, u32[]{:S(2)}, u32[]{:S(2)}) collective-permute-start(bf16[320,256]{1,0:T(8,128)(2,1)S(1)} %get-tuple-element.77), channel_id=1, source_target_pairs={{0,8},{12,4},{16,24},{28,20},{20,28},{1,9},{13,5},{17,25},{29,21},... | collective-permute-start | bytes 491528 | tf_op jit(solution)/shard_map/ppermute | solution.py:885
  414.2 8.4 %collective-permute-start.23 = (bf16[320,256]{1,0:T(8,128)(2,1)S(1)}, bf16[320,256]{1,0:T(8,128)(2,1)S(1)}, u32[]{:S(2)}, u32[]{:S(2)}) collective-permute-start(bf16[320,256]{1,0:T(8,128)(2,1)S(1)} %get-tuple-element.76), channel_id=1, source_target_pairs={{0,12},{12,0},{16,28},{28,16},{20,24},{1,13},{13,1},{17,29},{29,17... | collective-permute-start | bytes 491528 | tf_op jit(solution)/shard_map/ppermute | solution.py:885
  414.9 7.7 %collective-permute-start.24 = (bf16[320,256]{1,0:T(8,128)(2,1)S(1)}, bf16[320,256]{1,0:T(8,128)(2,1)S(1)}, u32[]{:S(2)}, u32[]{:S(2)}) collective-permute-start(bf16[320,256]{1,0:T(8,128)(2,1)S(1)} %get-tuple-element.75), channel_id=1, source_target_pairs={{0,16},{12,28},{16,0},{28,12},{20,4},{1,17},{13,29},{17,1},{29,13}... | collective-permute-start | bytes 491528 | tf_op jit(solution)/shard_map/ppermute | solution.py:885
  415.6 24.9 %collective-permute-start.25 = (bf16[320,256]{1,0:T(8,128)(2,1)S(1)}, bf16[320,256]{1,0:T(8,128)(2,1)S(1)}, u32[]{:S(2)}, u32[]{:S(2)}) collective-permute-start(bf16[320,256]{1,0:T(8,128)(2,1)S(1)} %get-tuple-element.74), channel_id=1, source_target_pairs={{0,20},{12,24},{16,4},{28,8},{20,0},{1,21},{13,25},{17,5},{29,9},{... | collective-permute-start | bytes 491528 | tf_op jit(solution)/shard_map/ppermute | solution.py:885
  419.1 21.7 %collective-permute-start.26 = (bf16[320,256]{1,0:T(8,128)(2,1)S(1)}, bf16[320,256]{1,0:T(8,128)(2,1)S(1)}, u32[]{:S(2)}, u32[]{:S(2)}) collective-permute-start(bf16[320,256]{1,0:T(8,128)(2,1)S(1)} %get-tuple-element.73), channel_id=1, source_target_pairs={{0,24},{12,20},{16,8},{28,4},{20,12},{1,25},{13,21},{17,9},{29,5},... | collective-permute-start | bytes 491528 | tf_op jit(solution)/shard_map/ppermute | solution.py:885
  420.4 38.0 %collective-permute-start.27 = (bf16[320,256]{1,0:T(8,128)(2,1)S(1)}, bf16[320,256]{1,0:T(8,128)(2,1)S(1)}, u32[]{:S(2)}, u32[]{:S(2)}) collective-permute-start(bf16[320,256]{1,0:T(8,128)(2,1)S(1)} %get-tuple-element.72), channel_id=1, source_target_pairs={{0,28},{12,16},{16,12},{28,0},{20,8},{1,29},{13,17},{17,13},{29,1}... | collective-permute-start | bytes 491528 | tf_op jit(solution)/shard_map/ppermute | solution.py:885
Sparse Core Ops, SparseCore 0:
  61.7 55.3 all-gather.7
  132.3 54.8 all-gather.5
  196.7 39.5 reduce-scatter.2
  245.3 33.2 reduce-scatter.4
  319.2 41.6 all-gather.9

commit v2 on v1

--- a/solution.py
+++ b/solution.py
@@ -18,6 +18,7 @@
 ROWS = (Z + H, Z + H, Z + H, H + E, H)
 PACK = 8
 CHUNK = 4
+FAR_FIRST = (4, 5, 6, 7, 2, 3, 1, 0)
 
 
 coeff_linear = 3.4445
@@ -853,12 +854,12 @@
             [jnp.pad(block, ((0, widest - block.shape[0]), (0, 0))) for block in ahead]
         )
         where = dp_index.astype(jnp.int32).reshape(1)
-        pieces = []
-        for step in range(dp_count):
+        pieces = [None] * dp_count
+        for step in FAR_FIRST:
             block = lax.dynamic_index_in_dim(blocks, kept[dp_index ^ step], 0, keepdims=False)
             if step > 0:
                 block = lax.ppermute(block, ("dz", "dx"), [(d ^ step, d) for d in owners])
-            pieces.append(block)
+            pieces[step] = block
         turned = run_collect(where, pieces, base)
     else:
         slots = [jnp.zeros((widest, units), bf16)] * dp_count
@@ -879,10 +880,10 @@
     )
     if dp_count == 8:
         dealt = run_deal(where, result, dp_count, base)
-        pieces = [dealt[0]]
-        for step in range(1, dp_count):
+        pieces = [dealt[0]] * dp_count
+        for step in FAR_FIRST[:-1]:
             pairs = [(d, d ^ step) for d in owners]
-            pieces.append(lax.ppermute(dealt[step], ("dz", "dx"), pairs))
+            pieces[step] = lax.ppermute(dealt[step], ("dz", "dx"), pairs)
         new_gru, new_post, new_prior = run_finish(owners, where, pieces, old_rows)
     else:
         result = result.T

time: 474 us -> 474 us (level)
  no operation moved by 1% of the time
where the time goes in v2:
time: 474 us; the launch traced here: 467 us
  Pallas kernels  188 us (40%)
  waiting for transfers between devices  103 us (22%)
  starting transfers between devices  48.6 us (10%)
  blocking collectives  38.9 us (8%)
  between operations  33.2 us (7%)
  local copies, waits for them, and re-layouts  27.6 us (6%)
  other arithmetic  18.6 us (4%)
  matrix products  9.53 us (2%)
    pallas_call x1, Pallas kernels, run_forward(): pl.pallas_call(functools.partial(scan_forward, seqs, CHUNK), out_shape=[j...  57.2 us
    pallas_call x1, Pallas kernels, run_backward(): pl.pallas_call(functools.partial(scan_backward, seqs, CHUNK), out_shape=j...  54.4 us
    pallas_call x1, Pallas kernels, run_orthogonal(): pl.pallas_call(functools.partial(orthogonal_block, base, 512), out_shape=...  47.7 us
    all_to_all x1, blocking collectives, exchange(): return lax.all_to_all(block, axis, 0, 0, tiled=True)  38.9 us
    ppermute x7, waiting for transfers between devices, on_device(): pieces[step] = lax.ppermute(dealt[step], ('dz', 'dx'), pairs)  37.9 us
    ppermute x7, starting transfers between devices, on_device(): block = lax.ppermute(block, ('dz', 'dx'), [(d ^ step, d) for d in owners])  21.4 us
    all_gather x3, waiting for transfers between devices, gather(): return lax.all_gather(block, 'tp', axis=0, tiled=False)  20.1 us
    reduce_scatter x2, waiting for transfers between devices, share_rows(): return lax.psum_scatter(block, 'dz', scatter_dimension=0, tiled=True)[0]  14.2 us
  transfers between devices with their start and end apart: 34, of which 15 were waited for; matrix products, arithmetic and copies ran while one was open for 9% of the time, Pallas kernels for 28%

profile of v2, /device:TPU:9, one launch (start us, length us, event | category | flops | bytes accessed | tf_op | source)
XLA Modules:
  0.0 467.5 jit_solution(6201714095543622610)
XLA Ops:
  7.2 2.1 slice.186.refs_0_
  9.3 1.3 collective-permute-start.1
  10.6 1.0 collective-permute-start
  12.4 1.2 collective-permute-start.3
  13.6 3.1 convert.16
  16.7 3.0 fusion.46
  22.2 1.5 copy.42
  23.8 4.7 %all-to-all-start = ((bf16[4,28,8,768]{3,2,1,0:T(8,128)(2,1)}), bf16[4,28,8,768]{3,2,1,0:T(8,128)(2,1)}, u32[]{:S(2)}, u32[]{:S(2)}) async-start(bf16[4,28,8,768]{3,2,1,0:T(8,128)(2,1)} %bitcast.7), calls=%async_computation | async-start | bytes 2752512 | tf_op jit(solution)/shard_map/all_to_all | solution.py:701
  30.2 1.9 convert_element_type.144
  32.1 12.6 %collective-permute-done.1.refs_2_ = bf16[3,1024,256]{2,1,0:T(8,128)(2,1)} collective-permute-done((bf16[3,1024,256]{2,1,0:T(8,128)(2,1)S(1)}, bf16[3,1024,256]{2,1,0:T(8,128)(2,1)}, u32[]{:S(2)}, u32[]{:S(2)}) %collective-permute-start.1) | collective-permute-done | bytes 1572896 | tf_op jit(solution)/shard_map/ppermute | solution.py:707
  44.7 2.7 collective-permute-start.2
  47.4 1.4 pad_maximum_fusion
  49.6 1.8 dynamic-slice_bitcast_fusion.t_ref
  52.7 2.4 collective-permute-start.6
  55.2 1.1 copy.43
  57.6 1.1 copy.44
  58.9 1.9 compare_convert_fusion
  62.6 57.2 %scan_forward.1 = (bf16[28,8,1024]{2,1,0:T(8,128)(2,1)}, f32[3,28,8,1024]{3,2,1,0:T(8,128)}, f32[28,8,1024]{2,1,0:T(8,128)}, bf16[3072,1024]{1,0:T(8,128)(2,1)}) custom-call(s32[1]{0:T(128)} %bitcast.spot_ref, bf16[4,28,8,768]{3,2,1,0:T(8,128)(2,1)} %all-to-all-done.x_ref, bf16[3,1024,256]{2,1,0:T(8,128)(2,1)} %copy-done.3, ...), custom_call_target="tpu_custom_call" | custom-call | flops 60000002048 | bytes 20971520 | tf_op jit(solution)/shard_map/scan_forward/pallas_call | solution.py:450
  119.8 1.3 collective-permute-start.12
  121.0 10.3 %heads.1 = (bf16[4,224,1024]{2,1,0:T(8,128)(2,1)}, f32[224,1024]{1,0:T(8,128)}, f32[1,1]{1,0:T(1,128)}) custom-call(s32[1]{0:T(128)} %bitcast.spot_ref, bf16[224,1024]{1,0:T(8,128)(2,1)} %bitcast.209, bf16[224,224]{1,0:T(8,128)(2,1)} %constant.146.clone.p_ref, bf16[224,1024]{1,0:T(8,128)(2,1)} %dynamic-slice_bitcast_fusion.t_ref, ...), custom_call_target="tpu_custom_call" | custom-call | flops 10000000000 | bytes 12582912 | tf_op jit(solution)/shard_map/heads/pallas_call | solution.py:506
  132.9 54.4 %scan_backward.1.earlier_ref = bf16[2,4,28,8,768]{4,3,2,1,0:T(8,128)(2,1)} custom-call(f32[28,8,1024]{2,1,0:T(8,128)} %bitcast.210, f32[3,28,8,1024]{3,2,1,0:T(8,128)} %get-tuple-element.47.k_hbm, f32[28,8,1024]{2,1,0:T(8,128)} %get-tuple-element.48.u_hbm, bf16[3072,1024]{1,0:T(8,128)(2,1)} %get-tuple-element.49.t_hbm), custom_call_target="tpu_custom_call" | custom-call | flops 60000002048 | bytes 20971520 | tf_op jit(solution)/shard_map/scan_backward/pallas_call | solution.py:481
  187.3 6.4 %head_grads.1 = bf16[3584,256]{1,0:T(8,128)(2,1)} custom-call(s32[2]{0:T(128)} %pad_add_fusion.1.spot_ref, f32[1]{0:T(128)} %bitcast.17.scale_ref, bf16[224,224]{1,0:T(8,128)(2,1)} %constant.146.clone.p_ref, bf16[4,4,224,1024]{3,2,1,0:T(8,128)(2,1)} %all-gather.6.cloned.1.call-done.r_hbm, bf16[4,224,1536]{2,1,0:T(8,128)(2,1)} %bitcast.207, ...), custom_call_target="tpu_custom_call" | custom-call | flops 4000000000 | bytes 12582912 | tf_op jit(solution)/shard_map/head_grads/pallas_call | solution.py:539
  193.7 1.0 slice-done.1
  195.2 1.4 pad_maximum_fusion.1.earlier_ref
  196.6 1.0 copy-done.2
  197.6 38.9 %all_to_all.10 = bf16[8,224,768]{2,1,0:T(8,128)(2,1)} all-to-all(bf16[8,224,768]{2,1,0:T(8,128)(2,1)S(1)} %bitcast.197), channel_id=1, replica_groups=mesh['dz'=4,'dx'=2,'tp'=4] {'dx','tp'}, dimensions={0} | all-to-all | bytes 5505024 | tf_op jit(solution)/shard_map/all_to_all | solution.py:701
  236.5 8.6 %gru_grads.1 = bf16[4,768,256]{2,1,0:T(8,128)(2,1)} custom-call(s32[2]{0:T(128)} %pad_add_fusion.1.spot_ref, f32[1]{0:T(128)} %bitcast.17.scale_ref, bf16[2,896,512]{2,1,0:T(8,128)(2,1)} %bitcast.194, bf16[4,4,224,1024]{3,2,1,0:T(8,128)(2,1)} %all-gather.6.cloned.1.call-done.r_hbm, bf16[2,4,224,768]{3,2,1,0:T(8,128)(2,1)} %bitcast.193, ...), custom_call_target="tpu_custom_call" | custom-call | flops 4000000000 | bytes 12582912 | tf_op jit(solution)/shard_map/gru_grads/pallas_call | solution.py:560
  245.3 1.0 dynamic-slice_bitcast_fusion.1
  262.8 1.6 add_convert_fusion.4
  264.4 14.2 %reduce-scatter.5.cloned.1.call-done = bf16[1,768,256]{2,1,0:T(8,128)(2,1)} async-done(((bf16[4,768,256]{2,1,0:T(8,128)(2,1)}), bf16[1,768,256]{2,1,0:T(8,128)(2,1)}) %reduce-scatter.5.cloned.1.call-update) | async-done | bytes 393232 | tf_op jit(solution)/shard_map/reduce_scatter | solution.py:800
  278.6 1.0 convert_element_type.154
  279.6 1.3 fusion.17
  281.0 1.8 fusion.16
  282.9 3.1 collective-permute-start.14
  285.9 2.1 collective-permute-start.15
  289.4 7.8 %collective-permute-start.18 = (bf16[320,256]{1,0:T(8,128)(2,1)S(1)}, bf16[320,256]{1,0:T(8,128)(2,1)S(1)}, u32[]{:S(2)}, u32[]{:S(2)}) collective-permute-start(bf16[320,256]{1,0:T(8,128)(2,1)S(1)} %get-tuple-element.82), channel_id=1, source_target_pairs={{20,0},{24,12},{4,16},{8,28},{0,20},{21,1},{25,13},{5,17},{9,29},{... | collective-permute-start | bytes 491528 | tf_op jit(solution)/shard_map/ppermute | solution.py:861
  297.2 1.3 collective-permute-start.19
  298.6 5.8 %collective-permute-start.20 = (bf16[320,256]{1,0:T(8,128)(2,1)S(1)}, bf16[320,256]{1,0:T(8,128)(2,1)S(1)}, u32[]{:S(2)}, u32[]{:S(2)}) collective-permute-start(bf16[320,256]{1,0:T(8,128)(2,1)S(1)} %get-tuple-element.80), channel_id=1, source_target_pairs={{28,0},{16,12},{12,16},{0,28},{8,20},{29,1},{17,13},{13,17},{1,29}... | collective-permute-start | bytes 491528 | tf_op jit(solution)/shard_map/ppermute | solution.py:861
  304.4 6.2 %collective-permute-done.18.refs_5_ = bf16[320,256]{1,0:T(8,128)(2,1)S(1)} collective-permute-done((bf16[320,256]{1,0:T(8,128)(2,1)S(1)}, bf16[320,256]{1,0:T(8,128)(2,1)S(1)}, u32[]{:S(2)}, u32[]{:S(2)}) %collective-permute-start.18) | collective-permute-done | bytes 163872 | tf_op jit(solution)/shard_map/ppermute | solution.py:861
  310.6 3.5 collective-permute-done.19.refs_6_
  314.1 3.5 collective-permute-done.20.refs_7_
  317.6 1.5 collect.1
  320.4 1.2 constant_dynamic-slice_fusion.2.refs_2_.refs_8_
  322.2 1.3 collective-permute-start.8
  323.5 1.0 constant_dynamic-slice_fusion.1.refs_3_.refs_9_
  326.4 1.5 collective-permute-done.9
  328.0 2.4 collective-permute-done.10
  330.4 1.7 collective-permute-start.11
  332.1 1.3 dynamic-slice_bitcast_fusion.5
  335.6 1.5 slice-done
  337.1 1.4 copy.48
  338.6 2.3 broadcast_multiply_fusion
  340.9 20.1 %all-gather.10.cloned.1.call-done.g_ref = bf16[1024,2560]{1,0:T(8,128)(2,1)} async-done(((bf16[256,2560]{1,0:T(8,128)(2,1)}), bf16[1024,2560]{1,0:T(8,128)(2,1)}) %all-gather.10.cloned.1.call-update) | async-done | bytes 5242896 | tf_op jit(solution)/shard_map/all_gather | solution.py:698
  360.9 2.5 copy-done
  363.4 47.7 %orthogonal.1.g_ref = bf16[256,2560]{1,0:T(8,128)(2,1)S(1)} custom-call(s32[2]{0:T(128)S(1)} %pad_add_fusion.own_ref, bf16[1024,2560]{1,0:T(8,128)(2,1)S(1)} %copy-done, f32[16,56,384]{2,1,0:T(8,128)S(1)} %bitcast.191, f32[1,1]{1,0:T(1,128)} %div.31.refs_1_, f32[3,256,256]{2,1,0:T(8,128)S(1)} %constant_dynamic-slice_fusion.2.refs_2_.refs_8_, ...), custom_call_target="tpu_custom_call" | custom-call | flops 49999998976 | bytes 6291456 | tf_op jit(solution)/shard_map/orthogonal/pallas_call | solution.py:594
  411.6 1.3 collective-permute-start.21
  412.9 1.3 collective-permute-start.22
  415.6 1.3 collective-permute-start.25
  416.9 2.2 collective-permute-done.21.refs_1_
  419.1 1.3 collective-permute-start.26
  420.4 1.3 collective-permute-start.27
  422.6 17.9 %collective-permute-done.25.refs_5_ = bf16[320,256]{1,0:T(8,128)(2,1)S(1)} collective-permute-done((bf16[320,256]{1,0:T(8,128)(2,1)S(1)}, bf16[320,256]{1,0:T(8,128)(2,1)S(1)}, u32[]{:S(2)}, u32[]{:S(2)}) %collective-permute-start.25) | collective-permute-done | bytes 163872 | tf_op jit(solution)/shard_map/ppermute | solution.py:886
  440.8 17.5 %collective-permute-done.27.refs_7_ = bf16[320,256]{1,0:T(8,128)(2,1)S(1)} collective-permute-done((bf16[320,256]{1,0:T(8,128)(2,1)S(1)}, bf16[320,256]{1,0:T(8,128)(2,1)S(1)}, u32[]{:S(2)}, u32[]{:S(2)}) %collective-permute-start.27) | collective-permute-done | bytes 163872 | tf_op jit(solution)/shard_map/ppermute | solution.py:886
  458.3 1.3 finish.1
  (107 shorter events, 22.4 us)
Async XLA Ops:
  7.2 4.4 copy-start.6
  9.3 7.5 %copy-start.3 = (bf16[3,1024,256]{2,1,0:T(8,128)(2,1)}, bf16[3,1024,256]{2,1,0:T(8,128)(2,1)S(1)}, u32[]{:S(2)}) copy-start(bf16[3,1024,256]{2,1,0:T(8,128)(2,1)S(1)} %slice.186.refs_0_) | copy-start | bytes 4718596
  9.3 35.4 %collective-permute-start.1 = (bf16[3,1024,256]{2,1,0:T(8,128)(2,1)S(1)}, bf16[3,1024,256]{2,1,0:T(8,128)(2,1)}, u32[]{:S(2)}, u32[]{:S(2)}) collective-permute-start(bf16[3,1024,256]{2,1,0:T(8,128)(2,1)S(1)} %slice.186.refs_0_), channel_id=1, source_target_pairs={{0,2},{1,3},{2,0},{3,1},{4,6},{5,7},{6,4},{7,5},{8,10},{9,11},{10,... | collective-permute-start | bytes 4718600 | tf_op jit(solution)/shard_map/ppermute | solution.py:707
  10.6 50.2 %collective-permute-start = (bf16[3,1024,256]{2,1,0:T(8,128)(2,1)S(1)}, bf16[3,1024,256]{2,1,0:T(8,128)(2,1)}, u32[]{:S(2)}, u32[]{:S(2)}) collective-permute-start(bf16[3,1024,256]{2,1,0:T(8,128)(2,1)S(1)} %slice.186.refs_0_), channel_id=1, source_target_pairs={{0,1},{1,0},{2,3},{3,2},{4,5},{5,4},{6,7},{7,6},{8,9},{9,8},{10,11... | collective-permute-start | bytes 4718600 | tf_op jit(solution)/shard_map/ppermute | solution.py:707
  12.4 45.2 %collective-permute-start.3 = (bf16[896,32]{1,0:T(8,128)(2,1)}, bf16[896,32]{1,0:T(8,128)(2,1)}, u32[]{:S(2)}, u32[]{:S(2)}) collective-permute-start(bf16[896,32]{1,0:T(8,128)(2,1)} %bitcast.3), channel_id=1, source_target_pairs={{0,4},{4,0},{1,5},{5,1},{2,6},{6,2},{3,7},{7,3},{8,12},{12,8},{9,1... | collective-permute-start | bytes 172040 | tf_op jit(solution)/shard_map/ppermute | solution.py:734
  23.8 4.7 %copy-start.8 = (s32[16]{0:T(128)S(1)}, s32[16]{0:T(128)}, u32[]{:S(2)}) copy-start(s32[16]{0:T(128)} %param.13) | copy-start | bytes 196
  23.8 6.4 %copy-start.4 = (f32[1024,256]{1,0:T(8,128)S(1)}, f32[1024,256]{1,0:T(8,128)}, u32[]{:S(2)}) copy-start(f32[1024,256]{1,0:T(8,128)} %param.16) | copy-start | bytes 3145732
  23.8 37.0 %all-to-all-start = ((bf16[4,28,8,768]{3,2,1,0:T(8,128)(2,1)}), bf16[4,28,8,768]{3,2,1,0:T(8,128)(2,1)}, u32[]{:S(2)}, u32[]{:S(2)}) async-start(bf16[4,28,8,768]{3,2,1,0:T(8,128)(2,1)} %bitcast.7), calls=%async_computation | async-start | bytes 2752512 | tf_op jit(solution)/shard_map/all_to_all | solution.py:701
  28.5 92.6 %all-gather.8.cloned.1.call-start = ((), (), s32[]{:S(2)}) async-start(), calls=%async_computation.7 | async-start | bytes 9175040 | tf_op jit(solution)/shard_map/all_gather | solution.py:698
  29.8 19.1 %collective-permute-start.4 = (f32[8,128]{1,0:T(8,128)S(1)}, f32[8,128]{1,0:T(8,128)S(1)}, u32[]{:S(2)}, u32[]{:S(2)}) collective-permute-start(f32[8,128]{1,0:T(8,128)S(1)} %broadcast_in_dim.7), channel_id=1, source_target_pairs={{0,4},{4,0},{1,5},{5,1},{2,6},{6,2},{3,7},{7,3},{8,12},{12,8},{9,1... | collective-permute-start | bytes 12296 | tf_op jit(solution)/shard_map/ppermute | solution.py:757
  44.7 16.1 %collective-permute-start.2 = (bf16[3,1024,256]{2,1,0:T(8,128)(2,1)}, bf16[3,1024,256]{2,1,0:T(8,128)(2,1)}, u32[]{:S(2)}, u32[]{:S(2)}) collective-permute-start(bf16[3,1024,256]{2,1,0:T(8,128)(2,1)} %collective-permute-done.1.refs_2_), channel_id=1, source_target_pairs={{0,1},{1,0},{2,3},{3,2},{4,5},{5,4},{6,7},{7,6},{8,9},{9,8},{10,11... | collective-permute-start | bytes 4718600 | tf_op jit(solution)/shard_map/ppermute | solution.py:707
  49.5 2.6 collective-permute-start.5
  52.7 3.5 collective-permute-start.6
  61.6 125.7 %all-gather.6.cloned.1.call-start = ((), (), s32[]{:S(2)}) async-start(), calls=%async_computation.4 | async-start | bytes 9175040 | tf_op jit(solution)/shard_map/all_gather | solution.py:698
  119.8 11.6 %collective-permute-start.12 = (bf16[224,1024]{1,0:T(8,128)(2,1)}, bf16[224,1024]{1,0:T(8,128)(2,1)S(1)}, u32[]{:S(2)}, u32[]{:S(2)}) collective-permute-start(bf16[224,1024]{1,0:T(8,128)(2,1)} %bitcast.208), channel_id=1, source_target_pairs={{0,4},{4,0},{1,5},{5,1},{2,6},{6,2},{3,7},{7,3},{8,12},{12,8},{9,1... | collective-permute-start | bytes 1376264 | tf_op jit(solution)/shard_map/ppermute | solution.py:767
  132.2 113.0 %reduce-scatter.3.cloned.1.call-start = ((), (), s32[]{:S(2)}) async-start(), calls=%async_computation.5 | async-start | bytes 2293760 | tf_op jit(solution)/shard_map/reduce_scatter | solution.py:800
  193.7 1.0 slice-start.1
  193.7 1.5 slice-start.2
  195.1 2.4 copy-start.2
  196.5 82.0 %reduce-scatter.5.cloned.1.call-start = ((), (), s32[]{:S(2)}) async-start(), calls=%async_computation.6 | async-start | bytes 1966080 | tf_op jit(solution)/shard_map/reduce_scatter | solution.py:800
  245.1 1.5 copy-start.7
  245.2 17.6 %copy-start.5 = (bf16[1,2,448,256]{3,2,1,0:T(8,128)(2,1)S(1)}, bf16[1,2,448,256]{3,2,1,0:T(8,128)(2,1)}, u32[]{:S(2)}) copy-start(bf16[1,2,448,256]{3,2,1,0:T(8,128)(2,1)} %reduce-scatter.3.cloned.1.call-done) | copy-start | bytes 1376260
  245.2 115.7 %all-gather.10.cloned.1.call-start = ((), (), s32[]{:S(2)}) async-start(), calls=%async_computation.8 | async-start | bytes 6553600 | tf_op jit(solution)/shard_map/all_gather | solution.py:698
  246.3 16.5 %collective-permute-start.13 = (bf16[448,256]{1,0:T(8,128)(2,1)S(1)}, bf16[448,256]{1,0:T(8,128)(2,1)S(1)}, u32[]{:S(2)}, u32[]{:S(2)}) collective-permute-start(bf16[448,256]{1,0:T(8,128)(2,1)S(1)} %dynamic-slice_bitcast_fusion.1), channel_id=1, source_target_pairs={{0,4},{4,0},{1,5},{5,1},{2,6},{6,2},{3,7},{7,3},{8,12},{12,8},{9,1... | collective-permute-start | bytes 688136 | tf_op jit(solution)/shard_map/ppermute | solution.py:811
  282.9 14.4 %collective-permute-start.14 = (bf16[320,256]{1,0:T(8,128)(2,1)S(1)}, bf16[320,256]{1,0:T(8,128)(2,1)S(1)}, u32[]{:S(2)}, u32[]{:S(2)}) collective-permute-start(bf16[320,256]{1,0:T(8,128)(2,1)S(1)} %get-tuple-element.86), channel_id=1, source_target_pairs={{4,0},{8,12},{20,16},{24,28},{16,20},{5,1},{9,13},{21,17},{25,29},... | collective-permute-start | bytes 491528 | tf_op jit(solution)/shard_map/ppermute | solution.py:861
  285.9 12.6 %collective-permute-start.15 = (bf16[320,256]{1,0:T(8,128)(2,1)S(1)}, bf16[320,256]{1,0:T(8,128)(2,1)S(1)}, u32[]{:S(2)}, u32[]{:S(2)}) collective-permute-start(bf16[320,256]{1,0:T(8,128)(2,1)S(1)} %get-tuple-element.85), channel_id=1, source_target_pairs={{8,0},{4,12},{24,16},{20,28},{28,20},{9,1},{5,13},{25,17},{21,29},... | collective-permute-start | bytes 491528 | tf_op jit(solution)/shard_map/ppermute | solution.py:861
  288.1 16.3 %collective-permute-start.16 = (bf16[320,256]{1,0:T(8,128)(2,1)S(1)}, bf16[320,256]{1,0:T(8,128)(2,1)S(1)}, u32[]{:S(2)}, u32[]{:S(2)}) collective-permute-start(bf16[320,256]{1,0:T(8,128)(2,1)S(1)} %get-tuple-element.84), channel_id=1, source_target_pairs={{12,0},{0,12},{28,16},{16,28},{24,20},{13,1},{1,13},{29,17},{17,29... | collective-permute-start | bytes 491528 | tf_op jit(solution)/shard_map/ppermute | solution.py:861
  288.7 15.6 %collective-permute-start.17 = (bf16[320,256]{1,0:T(8,128)(2,1)S(1)}, bf16[320,256]{1,0:T(8,128)(2,1)S(1)}, u32[]{:S(2)}, u32[]{:S(2)}) collective-permute-start(bf16[320,256]{1,0:T(8,128)(2,1)S(1)} %get-tuple-element.83), channel_id=1, source_target_pairs={{16,0},{28,12},{0,16},{12,28},{4,20},{17,1},{29,13},{1,17},{13,29}... | collective-permute-start | bytes 491528 | tf_op jit(solution)/shard_map/ppermute | solution.py:861
  289.4 21.2 %collective-permute-start.18 = (bf16[320,256]{1,0:T(8,128)(2,1)S(1)}, bf16[320,256]{1,0:T(8,128)(2,1)S(1)}, u32[]{:S(2)}, u32[]{:S(2)}) collective-permute-start(bf16[320,256]{1,0:T(8,128)(2,1)S(1)} %get-tuple-element.82), channel_id=1, source_target_pairs={{20,0},{24,12},{4,16},{8,28},{0,20},{21,1},{25,13},{5,17},{9,29},{... | collective-permute-start | bytes 491528 | tf_op jit(solution)/shard_map/ppermute | solution.py:861
  297.2 16.9 %collective-permute-start.19 = (bf16[320,256]{1,0:T(8,128)(2,1)S(1)}, bf16[320,256]{1,0:T(8,128)(2,1)S(1)}, u32[]{:S(2)}, u32[]{:S(2)}) collective-permute-start(bf16[320,256]{1,0:T(8,128)(2,1)S(1)} %get-tuple-element.81), channel_id=1, source_target_pairs={{24,0},{20,12},{8,16},{4,28},{12,20},{25,1},{21,13},{9,17},{5,29},... | collective-permute-start | bytes 491528 | tf_op jit(solution)/shard_map/ppermute | solution.py:861
  298.6 19.0 %collective-permute-start.20 = (bf16[320,256]{1,0:T(8,128)(2,1)S(1)}, bf16[320,256]{1,0:T(8,128)(2,1)S(1)}, u32[]{:S(2)}, u32[]{:S(2)}) collective-permute-start(bf16[320,256]{1,0:T(8,128)(2,1)S(1)} %get-tuple-element.80), channel_id=1, source_target_pairs={{28,0},{16,12},{12,16},{0,28},{8,20},{29,1},{17,13},{13,17},{1,29}... | collective-permute-start | bytes 491528 | tf_op jit(solution)/shard_map/ppermute | solution.py:861
  319.7 1.8 collective-permute-start.7
  322.2 2.5 collective-permute-start.8
  325.4 2.5 collective-permute-start.9
  327.9 2.5 collective-permute-start.10
  330.4 3.4 collective-permute-start.11
  335.6 1.5 slice-start
  340.9 70.3 %copy-start.1 = (f32[4,4,56,384]{3,2,1,0:T(8,128)}, f32[4,4,56,384]{3,2,1,0:T(8,128)S(1)}, u32[]{:S(2)}) copy-start(f32[4,4,56,384]{3,2,1,0:T(8,128)S(1)} %broadcast_multiply_fusion) | copy-start | bytes 4128772
  360.9 2.5 copy-start
  411.6 7.4 %collective-permute-start.21 = (bf16[320,256]{1,0:T(8,128)(2,1)S(1)}, bf16[320,256]{1,0:T(8,128)(2,1)S(1)}, u32[]{:S(2)}, u32[]{:S(2)}) collective-permute-start(bf16[320,256]{1,0:T(8,128)(2,1)S(1)} %get-tuple-element.78), channel_id=1, source_target_pairs={{0,4},{12,8},{16,20},{28,24},{20,16},{1,5},{13,9},{17,21},{29,25},... | collective-permute-start | bytes 491528 | tf_op jit(solution)/shard_map/ppermute | solution.py:886
  412.9 7.4 %collective-permute-start.22 = (bf16[320,256]{1,0:T(8,128)(2,1)S(1)}, bf16[320,256]{1,0:T(8,128)(2,1)S(1)}, u32[]{:S(2)}, u32[]{:S(2)}) collective-permute-start(bf16[320,256]{1,0:T(8,128)(2,1)S(1)} %get-tuple-element.77), channel_id=1, source_target_pairs={{0,8},{12,4},{16,24},{28,20},{20,28},{1,9},{13,5},{17,25},{29,21},... | collective-permute-start | bytes 491528 | tf_op jit(solution)/shard_map/ppermute | solution.py:886
  414.2 8.4 %collective-permute-start.23 = (bf16[320,256]{1,0:T(8,128)(2,1)S(1)}, bf16[320,256]{1,0:T(8,128)(2,1)S(1)}, u32[]{:S(2)}, u32[]{:S(2)}) collective-permute-start(bf16[320,256]{1,0:T(8,128)(2,1)S(1)} %get-tuple-element.76), channel_id=1, source_target_pairs={{0,12},{12,0},{16,28},{28,16},{20,24},{1,13},{13,1},{17,29},{29,17... | collective-permute-start | bytes 491528 | tf_op jit(solution)/shard_map/ppermute | solution.py:886
  414.9 7.7 %collective-permute-start.24 = (bf16[320,256]{1,0:T(8,128)(2,1)S(1)}, bf16[320,256]{1,0:T(8,128)(2,1)S(1)}, u32[]{:S(2)}, u32[]{:S(2)}) collective-permute-start(bf16[320,256]{1,0:T(8,128)(2,1)S(1)} %get-tuple-element.75), channel_id=1, source_target_pairs={{0,16},{12,28},{16,0},{28,12},{20,4},{1,17},{13,29},{17,1},{29,13}... | collective-permute-start | bytes 491528 | tf_op jit(solution)/shard_map/ppermute | solution.py:886
  415.6 24.9 %collective-permute-start.25 = (bf16[320,256]{1,0:T(8,128)(2,1)S(1)}, bf16[320,256]{1,0:T(8,128)(2,1)S(1)}, u32[]{:S(2)}, u32[]{:S(2)}) collective-permute-start(bf16[320,256]{1,0:T(8,128)(2,1)S(1)} %get-tuple-element.74), channel_id=1, source_target_pairs={{0,20},{12,24},{16,4},{28,8},{20,0},{1,21},{13,25},{17,5},{29,9},{... | collective-permute-start | bytes 491528 | tf_op jit(solution)/shard_map/ppermute | solution.py:886
  419.1 21.7 %collective-permute-start.26 = (bf16[320,256]{1,0:T(8,128)(2,1)S(1)}, bf16[320,256]{1,0:T(8,128)(2,1)S(1)}, u32[]{:S(2)}, u32[]{:S(2)}) collective-permute-start(bf16[320,256]{1,0:T(8,128)(2,1)S(1)} %get-tuple-element.73), channel_id=1, source_target_pairs={{0,24},{12,20},{16,8},{28,4},{20,12},{1,25},{13,21},{17,9},{29,5},... | collective-permute-start | bytes 491528 | tf_op jit(solution)/shard_map/ppermute | solution.py:886
  420.4 38.0 %collective-permute-start.27 = (bf16[320,256]{1,0:T(8,128)(2,1)S(1)}, bf16[320,256]{1,0:T(8,128)(2,1)S(1)}, u32[]{:S(2)}, u32[]{:S(2)}) collective-permute-start(bf16[320,256]{1,0:T(8,128)(2,1)S(1)} %get-tuple-element.72), channel_id=1, source_target_pairs={{0,28},{12,16},{16,12},{28,0},{20,8},{1,29},{13,17},{17,13},{29,1}... | collective-permute-start | bytes 491528 | tf_op jit(solution)/shard_map/ppermute | solution.py:886
Sparse Core Ops, SparseCore 0:
  61.7 55.3 all-gather.7
  132.3 54.8 all-gather.5
  196.7 39.5 reduce-scatter.2
  245.3 33.2 reduce-scatter.4
  319.2 41.6 all-gather.9
